TPU v7x, 32 devices: a whole 2x2x4 slice. The times are simulated.
32 devices in a mesh: fsdp: 4 (over y, x), seq: 8 (over z, core).
Axes of the slice: x: 2, y: 2, z: 4, core: 2. Of those that a mesh axis runs over, the one named last changes fastest.
Arguments:
- tokens: bfloat16 [4, 1024, 1600], P('fsdp', 'seq'), may hold values from -6 to 6
- segment_ids: int32 [4, 1024], P('fsdp', 'seq'), may hold values from 0 to 7, never falling along the last dimension, each value on 1 to 512 neighbouring positions
- cotangent: bfloat16 [4, 1024, 1600], P('fsdp', 'seq'), may hold values from -6 to 6
- qkv_weight: bfloat16 [1600, 4800], P('fsdp', 'seq'), may hold values from -0.15625 to 0.15625
- attn_out_weight: bfloat16 [1600, 1600], P('fsdp', 'seq'), may hold values from -1.25 to 1.25
- fc_weight: bfloat16 [1600, 6400], P(None, ('fsdp', 'seq')), may hold values from -0.15625 to 0.15625
- proj_weight: bfloat16 [6400, 1600], P(('fsdp', 'seq')), may hold values from -0.078125 to 0.078125
- vectors: bfloat16 [8, 1600], P('fsdp', 'seq'), may hold values from -1.5 to 1.5
- fc_bias: bfloat16 [6400], P(('fsdp', 'seq')), may hold values from -2 to 2
Outputs:
- output: float32 [4, 1024, 1600], P('fsdp', 'seq')
- input_grad: float32 [4, 1024, 1600], P('fsdp', 'seq')
- grad_qkv: float32 [1600, 4800], P('fsdp', 'seq')
- grad_attn_out: float32 [1600, 1600], P('fsdp', 'seq')
- grad_fc: float32 [1600, 6400], P(None, ('fsdp', 'seq'))
- grad_proj: float32 [6400, 1600], P(('fsdp', 'seq'))
- grad_vectors: float32 [8, 1600], P('fsdp', 'seq')
- grad_fc_bias: float32 [6400], P(('fsdp', 'seq'))
Inputs may be any that keep to these rules, and one draw needn't show every extreme that they name: `segment_ids`: along each sequence the ids never fall, and each document holds at most 512 tokens.
All inputs are finite; a program needn't handle non-finite values.
Results may differ from a plain program's by a relative error of at most 0.019.
Values may be sent and summed in bfloat16 or wider, within the bound.
A program may use at most 384 MiB of HBM per device.

v0:
```python
import math

import jax
import jax.numpy as jnp
from jax import lax
from jax.sharding import PartitionSpec as P

HEADS = 25
HEAD_DIM = 64


norm_eps = 1e-05
tanh_coeff = math.sqrt(2.0 / math.pi)
cubic_coeff = 0.044715
masked_score = -1e30


def layer_norm(values, gain, shift):
    centred = values - jnp.mean(values, axis=-1, keepdims=True)
    inverse = lax.rsqrt(jnp.mean(centred * centred, axis=-1, keepdims=True) + norm_eps)
    normed = centred * inverse
    return (normed, inverse, normed * gain + shift)


def norm_back(grad_out, normed, inverse, gain):
    scaled = grad_out * gain
    grad_in = inverse * (
        scaled
        - jnp.mean(scaled, axis=-1, keepdims=True)
        - normed * jnp.mean(scaled * normed, axis=-1, keepdims=True)
    )
    return (grad_in, jnp.sum(grad_out * normed, axis=0), jnp.sum(grad_out, axis=0))


def gelu_parts(preact):
    inner = tanh_coeff * (preact + cubic_coeff * preact * preact * preact)
    tangent = jnp.tanh(inner)
    gelu_value = 0.5 * preact * (1.0 + tangent)
    gelu_slope = 0.5 * (1.0 + tangent) + 0.5 * preact * (1.0 - tangent * tangent) * tanh_coeff * (
        1.0 + 3.0 * cubic_coeff * preact * preact
    )
    return (gelu_value, gelu_slope)


def block_rows():
    return 512


def gather_owned(matrix_qkv, matrix_attn, matrix_fc, matrix_proj, vector_part, bias_part):
    return (
        lax.all_gather(matrix_qkv, "fsdp", axis=0, tiled=True),
        lax.all_gather(matrix_attn, "fsdp", axis=0, tiled=True),
        lax.all_gather(matrix_fc, "fsdp", axis=1, tiled=True),
        lax.all_gather(matrix_proj, "fsdp", axis=0, tiled=True),
        lax.all_gather(vector_part, "fsdp", axis=0, tiled=True),
        lax.all_gather(bias_part, "fsdp", axis=0, tiled=True),
    )


def gather_attention(matrix_qkv, matrix_attn, vector_part, id_part):
    return (
        lax.all_gather(matrix_qkv, "seq", axis=1, tiled=True),
        lax.all_gather(matrix_attn, "seq", axis=1, tiled=True),
        lax.all_gather(vector_part, "seq", axis=1, tiled=True),
        lax.all_gather(id_part, "seq", axis=0, tiled=True),
    )


def per_device(
    tokens,
    segment_ids,
    cotangent,
    qkv_weight,
    attn_out_weight,
    fc_weight,
    proj_weight,
    vectors,
    fc_bias,
):
    width = tokens.shape[2]
    local_rows = tokens.shape[1]
    heads = HEADS
    head_width = HEAD_DIM
    score_scale = head_width ** (-0.5)
    own_index = lax.axis_index("seq")
    inputs_bf = tokens[0]
    inputs = inputs_bf.astype(jnp.float32)
    doc_ids = segment_ids[0].astype(jnp.bfloat16)
    grad_out_bf = cotangent[0]
    owned = gather_owned(qkv_weight, attn_out_weight, fc_weight, proj_weight, vectors, fc_bias)
    w_qkv, w_attn, vector_bf, ids_all = gather_attention(owned[0], owned[1], owned[4], doc_ids)

    def gather_feedforward(matrix_fc, matrix_proj, bias_part):
        return (
            lax.all_gather(matrix_fc, "seq", axis=1, tiled=True),
            lax.all_gather(matrix_proj, "seq", axis=0, tiled=True),
            lax.all_gather(bias_part, "seq", axis=0, tiled=True),
        )

    w_fc, w_proj, bias_units = gather_feedforward(owned[2], owned[3], owned[5])
    vector_rows = vector_bf.astype(jnp.float32)
    fc_shift = bias_units.astype(jnp.float32)
    normed1, inverse1, shifted1 = layer_norm(inputs, vector_rows[0], vector_rows[1])
    hidden1 = shifted1.astype(jnp.bfloat16)
    projected = jnp.dot(hidden1, w_qkv, preferred_element_type=jnp.float32)
    queries = (projected[:, :width] + vector_rows[2]).astype(jnp.bfloat16)
    keys_own = projected[:, width : 2 * width].astype(jnp.bfloat16)
    values_own = (projected[:, 2 * width :] + vector_rows[3]).astype(jnp.bfloat16)
    query_heads = queries.reshape(local_rows, heads, head_width)
    positions = own_index * local_rows + lax.iota(jnp.int32, local_rows)

    def scores_for(key_block, ids_block, pos_block):
        scores = (
            jnp.einsum("qhd,khd->hqk", query_heads, key_block, preferred_element_type=jnp.float32)
            * score_scale
        )
        allowed = (
            (pos_block[None, :] <= positions[:, None])
            & (pos_block[None, :] >= 0)
            & (ids_block[None, :] == doc_ids[:, None])
        )
        return (scores, allowed)

    def stat_step(running, block_items):
        running_max, running_sum = running
        key_block, value_block, ids_block, pos_block = block_items
        scores, allowed = scores_for(key_block, ids_block, pos_block)
        masked = jnp.where(allowed[None], scores, masked_score)
        new_max = jnp.maximum(running_max, jnp.max(masked, axis=2))
        fading = jnp.exp(running_max - new_max)
        weights = jnp.where(allowed[None], jnp.exp(masked - new_max[:, :, None]), 0.0)
        running_sum = running_sum * fading + jnp.sum(weights, axis=2)
        return ((new_max, running_sum), None)

    initial = (
        jnp.full((heads, local_rows), masked_score, jnp.float32),
        jnp.zeros((heads, local_rows), jnp.float32),
    )
    keys_all, values_all = (
        lax.all_gather(keys_own, "seq", axis=0, tiled=True),
        lax.all_gather(values_own, "seq", axis=0, tiled=True),
    )
    key_count = keys_all.shape[0]
    step_rows = block_rows()
    blocks = key_count // step_rows
    key_items = (
        keys_all.reshape(blocks, step_rows, heads, head_width),
        values_all.reshape(blocks, step_rows, heads, head_width),
        ids_all.reshape(blocks, step_rows),
        lax.iota(jnp.int32, key_count).reshape(blocks, step_rows),
    )
    running, _ = lax.scan(stat_step, initial, key_items)
    final_max, final_sum = running
    log_total = final_max + jnp.log(final_sum)

    def weigh_step(total, block_items):
        key_block, value_block, ids_block, pos_block = block_items
        scores, allowed = scores_for(key_block, ids_block, pos_block)
        probs_bf = jnp.where(allowed[None], jnp.exp(scores - log_total[:, :, None]), 0.0).astype(
            jnp.bfloat16
        )
        return (
            total
            + jnp.einsum("hqk,khd->hqd", probs_bf, value_block, preferred_element_type=jnp.float32),
            None,
        )

    final_acc, _ = lax.scan(
        weigh_step, jnp.zeros((heads, local_rows, head_width), jnp.float32), key_items
    )
    attn_bf = final_acc.astype(jnp.bfloat16).transpose(1, 0, 2).reshape(local_rows, width)
    resid = inputs + jnp.dot(attn_bf, w_attn, preferred_element_type=jnp.float32) + vector_rows[4]
    normed2, inverse2, shifted2 = layer_norm(resid, vector_rows[5], vector_rows[6])
    hidden2 = shifted2.astype(jnp.bfloat16)
    preact = jnp.dot(hidden2, w_fc, preferred_element_type=jnp.float32) + fc_shift
    gelu_value, gelu_slope = gelu_parts(preact)
    act_bf = gelu_value.astype(jnp.bfloat16)
    mlp_out = jnp.dot(act_bf, w_proj, preferred_element_type=jnp.float32)
    result = resid + mlp_out + vector_rows[7]
    fenced = lax.optimization_barrier(
        (qkv_weight, attn_out_weight, fc_weight, proj_weight, vectors, fc_bias, doc_ids, result)
    )
    owned_again = gather_owned(fenced[0], fenced[1], fenced[2], fenced[3], fenced[4], fenced[5])
    back_qkv, back_attn, back_vec_bf, ids_again = gather_attention(
        owned_again[0], owned_again[1], owned_again[4], fenced[6]
    )
    back_fc, back_proj, bias_again = gather_feedforward(
        owned_again[2], owned_again[3], owned_again[5]
    )
    back_vec = back_vec_bf.astype(jnp.float32)
    grad_out = grad_out_bf.astype(jnp.float32)
    grad_proj_full = jnp.einsum(
        "tf,td->fd", act_bf, grad_out_bf, preferred_element_type=jnp.float32
    )
    grad_act = jnp.einsum("td,fd->tf", grad_out_bf, back_proj, preferred_element_type=jnp.float32)
    grad_pre = grad_act * gelu_slope
    grad_pre_bf = grad_pre.astype(jnp.bfloat16)
    grad_fc_full = jnp.einsum("td,tf->df", hidden2, grad_pre_bf, preferred_element_type=jnp.float32)
    grad_hidden2 = jnp.einsum("tf,df->td", grad_pre_bf, back_fc, preferred_element_type=jnp.float32)
    bias_full = jnp.sum(grad_pre, axis=0)
    part_fc, part_proj, part_bias = (
        lax.psum_scatter(
            grad_fc_full.astype(jnp.bfloat16), "seq", scatter_dimension=1, tiled=True
        ).astype(jnp.float32),
        lax.psum_scatter(
            grad_proj_full.astype(jnp.bfloat16), "seq", scatter_dimension=0, tiled=True
        ).astype(jnp.float32),
        lax.psum_scatter(
            bias_full.astype(jnp.bfloat16), "seq", scatter_dimension=0, tiled=True
        ).astype(jnp.float32),
    )
    grad_resid_norm, gain2_grad, shift2_grad = norm_back(
        grad_hidden2, normed2, inverse2, back_vec[5]
    )
    grad_resid = grad_out + grad_resid_norm
    grad_resid_bf = grad_resid.astype(jnp.bfloat16)
    grad_attn_out_full = jnp.einsum(
        "tc,td->cd", attn_bf, grad_resid_bf, preferred_element_type=jnp.float32
    )
    grad_attn_bf = jnp.einsum(
        "td,cd->tc", grad_resid_bf, back_attn, preferred_element_type=jnp.float32
    ).astype(jnp.bfloat16)
    grad_heads = grad_attn_bf.reshape(local_rows, heads, head_width)
    attn_heads = attn_bf.reshape(local_rows, heads, head_width)
    delta = jnp.sum(grad_heads.astype(jnp.float32) * attn_heads.astype(jnp.float32), axis=2).T

    def back_step(grad_query, block_items):
        key_block, value_block, ids_block, pos_block = block_items
        scores, allowed = scores_for(key_block, ids_block, pos_block)
        probs = jnp.where(allowed[None], jnp.exp(scores - log_total[:, :, None]), 0.0)
        probs_bf = probs.astype(jnp.bfloat16)
        value_grad = jnp.einsum(
            "hqk,qhd->khd", probs_bf, grad_heads, preferred_element_type=jnp.float32
        )
        prob_grad = jnp.einsum(
            "qhd,khd->hqk", grad_heads, value_block, preferred_element_type=jnp.float32
        )
        score_grad = (probs * (prob_grad - delta[:, :, None])).astype(jnp.bfloat16)
        grad_query = grad_query + score_scale * jnp.einsum(
            "hqk,khd->qhd", score_grad, key_block, preferred_element_type=jnp.float32
        )
        key_grad = score_scale * jnp.einsum(
            "hqk,qhd->khd", score_grad, query_heads, preferred_element_type=jnp.float32
        )
        return (grad_query, (key_grad, value_grad))

    query_zero = jnp.zeros((local_rows, heads, head_width), jnp.float32)
    grad_query, stacked_grads = lax.scan(back_step, query_zero, key_items)
    key_terms = stacked_grads[0].reshape(key_count, width)
    value_terms = stacked_grads[1].reshape(key_count, width)
    key_own_grad, value_own_grad = (
        lax.psum_scatter(
            key_terms.astype(jnp.bfloat16), "seq", scatter_dimension=0, tiled=True
        ).astype(jnp.float32),
        lax.psum_scatter(
            value_terms.astype(jnp.bfloat16), "seq", scatter_dimension=0, tiled=True
        ).astype(jnp.float32),
    )
    query_grad = grad_query.reshape(local_rows, width)
    grad_qkv_bf = jnp.concatenate([query_grad, key_own_grad, value_own_grad], axis=1).astype(
        jnp.bfloat16
    )
    grad_qkv_full = jnp.einsum(
        "td,te->de", hidden1, grad_qkv_bf, preferred_element_type=jnp.float32
    )
    grad_hidden1 = jnp.einsum(
        "te,de->td", grad_qkv_bf, back_qkv, preferred_element_type=jnp.float32
    )
    grad_input_norm, gain1_grad, shift1_grad = norm_back(
        grad_hidden1, normed1, inverse1, back_vec[0]
    )
    input_grad = grad_resid + grad_input_norm
    vector_grad = jnp.stack(
        [
            gain1_grad,
            shift1_grad,
            jnp.sum(query_grad, axis=0),
            jnp.sum(value_own_grad, axis=0),
            jnp.sum(grad_resid, axis=0),
            gain2_grad,
            shift2_grad,
            jnp.sum(grad_out, axis=0),
        ]
    )
    part_qkv, part_attn, part_vec = (
        lax.psum_scatter(
            grad_qkv_full.astype(jnp.bfloat16), "seq", scatter_dimension=1, tiled=True
        ).astype(jnp.float32),
        lax.psum_scatter(
            grad_attn_out_full.astype(jnp.bfloat16), "seq", scatter_dimension=1, tiled=True
        ).astype(jnp.float32),
        lax.psum_scatter(
            vector_grad.astype(jnp.bfloat16), "seq", scatter_dimension=1, tiled=True
        ).astype(jnp.float32),
    )
    own_qkv, own_attn, own_fc, own_proj, own_vec, own_bias = (
        lax.psum_scatter(
            part_qkv.astype(jnp.bfloat16), "fsdp", scatter_dimension=0, tiled=True
        ).astype(jnp.float32),
        lax.psum_scatter(
            part_attn.astype(jnp.bfloat16), "fsdp", scatter_dimension=0, tiled=True
        ).astype(jnp.float32),
        lax.psum_scatter(
            part_fc.astype(jnp.bfloat16), "fsdp", scatter_dimension=1, tiled=True
        ).astype(jnp.float32),
        lax.psum_scatter(
            part_proj.astype(jnp.bfloat16), "fsdp", scatter_dimension=0, tiled=True
        ).astype(jnp.float32),
        lax.psum_scatter(
            part_vec.astype(jnp.bfloat16), "fsdp", scatter_dimension=0, tiled=True
        ).astype(jnp.float32),
        lax.psum_scatter(
            part_bias.astype(jnp.bfloat16), "fsdp", scatter_dimension=0, tiled=True
        ).astype(jnp.float32),
    )
    return (result[None], input_grad[None], own_qkv, own_attn, own_fc, own_proj, own_vec, own_bias)


def solution(mesh):
    in_specs = (
        P("fsdp", "seq", None),
        P("fsdp", "seq"),
        P("fsdp", "seq", None),
        P("fsdp", "seq"),
        P("fsdp", "seq"),
        P(None, ("fsdp", "seq")),
        P(("fsdp", "seq"), None),
        P("fsdp", "seq"),
        P(("fsdp", "seq")),
    )
    out_specs = (
        P("fsdp", "seq", None),
        P("fsdp", "seq", None),
        P("fsdp", "seq"),
        P("fsdp", "seq"),
        P(None, ("fsdp", "seq")),
        P(("fsdp", "seq"), None),
        P("fsdp", "seq"),
        P(("fsdp", "seq")),
    )
    return jax.shard_map(
        per_device, mesh=mesh, in_specs=in_specs, out_specs=out_specs, check_vma=False
    )
```

profile of v0, /device:TPU:0, one launch (start us, length us, event | category | flops | bytes accessed | tf_op | source)
XLA Modules:
  0.0 2497.9 jit_solution(16197296727634834088)
XLA Ops:
  8.0 39.5 %all-gather.22.cloned.1.call-done = bf16[1600,600]{1,0:T(8,128)(2,1)} async-done(((bf16[400,600]{1,0:T(8,128)(2,1)}), bf16[1600,600]{1,0:T(8,128)(2,1)}) %all-gather.22.cloned.1.call-update) | async-done | bytes 1920016 | tf_op jit(solution)/shard_map/all_gather | solution.py:51
  79.7 116.8 %all-gather.24.cloned.1.call-done = bf16[1600,4800]{0,1:T(8,128)(2,1)} async-done(((bf16[1600,600]{0,1:T(8,128)(2,1)}), bf16[1600,4800]{0,1:T(8,128)(2,1)}) %all-gather.24.cloned.1.call-update) | async-done | bytes 15360016 | tf_op jit(solution)/shard_map/all_gather | solution.py:62
  240.2 41.6 %all-gather.36.cloned.1.call-done = bf16[800,1600]{1,0:T(8,128)(2,1)} async-done(((bf16[200,1600]{1,0:T(8,128)(2,1)}), bf16[800,1600]{1,0:T(8,128)(2,1)}) %all-gather.36.cloned.1.call-update) | async-done | bytes 2560016 | tf_op jit(solution)/shard_map/all_gather | solution.py:54
  305.0 26.8 %all-reduce.1 = bf16[6400]{0:T(1024)(128)(2,1)S(1)} all-reduce(bf16[6400]{0:T(1024)(128)(2,1)S(1)} %dynamic-update-slice.1), channel_id=1, replica_groups=mesh['fsdp'=4,'seq'=8] {'seq'}, use_global_device_ids=true, to_apply=%add.1 | all-reduce | flops 6400 | bytes 25600
  427.7 183.2 %all-gather.34.cloned.1.call-done = bf16[1600,6400]{0,1:T(8,128)(2,1)} async-done(((bf16[1600,800]{0,1:T(8,128)(2,1)}), bf16[1600,6400]{0,1:T(8,128)(2,1)}) %all-gather.34.cloned.1.call-update) | async-done | bytes 20480016 | tf_op jit(solution)/shard_map/all_gather | solution.py:95
  624.2 174.7 %all-gather.38.cloned.1.call-done = bf16[6400,1600]{1,0:T(8,128)(2,1)} async-done(((bf16[800,1600]{1,0:T(8,128)(2,1)}), bf16[6400,1600]{1,0:T(8,128)(2,1)}) %all-gather.38.cloned.1.call-update) | async-done | bytes 20480016 | tf_op jit(solution)/shard_map/all_gather | solution.py:96
  814.4 37.5 %all-gather.40.cloned.1.call-done = bf16[800,1600]{1,0:T(8,128)(2,1)} async-done(((bf16[200,1600]{1,0:T(8,128)(2,1)}), bf16[800,1600]{1,0:T(8,128)(2,1)}) %all-gather.40.cloned.1.call-update) | async-done | bytes 2560016 | tf_op jit(solution)/shard_map/all_gather | solution.py:54
  852.0 41.8 %all-gather.44.cloned.1.call-done = bf16[1600,800]{0,1:T(8,128)(2,1)} async-done(((bf16[1600,200]{0,1:T(8,128)(2,1)}), bf16[1600,800]{0,1:T(8,128)(2,1)}) %all-gather.44.cloned.1.call-update) | async-done | bytes 2560016 | tf_op jit(solution)/shard_map/all_gather | solution.py:53
  916.5 23.1 all-gather.4
  940.3 143.4 %all-gather.42.cloned.1.call-done = bf16[6400,1600]{1,0:T(8,128)(2,1)} async-done(((bf16[800,1600]{1,0:T(8,128)(2,1)}), bf16[6400,1600]{1,0:T(8,128)(2,1)}) %all-gather.42.cloned.1.call-update) | async-done | bytes 20480016 | tf_op jit(solution)/shard_map/all_gather | solution.py:96
  1098.0 173.7 %all-gather.46.cloned.1.call-done = bf16[1600,6400]{0,1:T(8,128)(2,1)} async-done(((bf16[1600,800]{0,1:T(8,128)(2,1)}), bf16[1600,6400]{0,1:T(8,128)(2,1)}) %all-gather.46.cloned.1.call-update) | async-done | bytes 20480016 | tf_op jit(solution)/shard_map/all_gather | solution.py:95
  1290.0 38.2 %all-gather.48.cloned.1.call-done = bf16[1600,1600]{0,1:T(8,128)(2,1)} async-done(((bf16[1600,200]{0,1:T(8,128)(2,1)}), bf16[1600,1600]{0,1:T(8,128)(2,1)}) %all-gather.48.cloned.1.call-update) | async-done | bytes 5120016 | tf_op jit(solution)/shard_map/all_gather | solution.py:63
  1334.0 32.0 %while.41 = (s32[]{:T(128)}, f32[128,25,64]{0,2,1:T(8,128)}, bf16[2,512,25,64]{1,3,2,0:T(8,128)(2,1)}, bf16[2,512,25,64]{1,3,2,0:T(8,128)(2,1)}, bf16[2,512,25,6...) while((s32[]{:T(128)}, f32[128,25,64]{0,2,1:T(8,128)}, ...), condition=%wide.region_14.15_spmd.clone, body=%wide.region_13.14_spmd.clone.sunk | while | flops 1066787456 | bytes 139519632 | solution.py:248
  1418.6 42.2 %reduce-scatter.30.cloned.1.call-done = bf16[128,1600]{1,0:T(8,128)(2,1)} async-done(((bf16[1024,1600]{1,0:T(8,128)(2,1)}), bf16[128,1600]{1,0:T(8,128)(2,1)}) %reduce-scatter.30.cloned.1.call-update) | async-done | bytes 409616
  1487.7 185.3 %reduce-scatter.28.cloned.1.call-done = bf16[800,1600]{1,0:T(8,128)(2,1)} async-done(((bf16[6400,1600]{1,0:T(8,128)(2,1)}), bf16[800,1600]{1,0:T(8,128)(2,1)}) %reduce-scatter.28.cloned.1.call-update) | async-done | bytes 2560016 | tf_op jit(solution)/shard_map/reduce_scatter | solution.py:205
  1673.1 34.9 %all-gather.50.cloned.1.call-done = bf16[1600,600]{1,0:T(8,128)(2,1)} async-done(((bf16[400,600]{1,0:T(8,128)(2,1)}), bf16[1600,600]{1,0:T(8,128)(2,1)}) %all-gather.50.cloned.1.call-update) | async-done | bytes 1920016 | tf_op jit(solution)/shard_map/all_gather | solution.py:51
  1712.2 59.4 %reduce-scatter.38.cloned.1.call-done = bf16[1600,200]{0,1:T(8,128)(2,1)} async-done(((bf16[1600,1600]{0,1:T(8,128)(2,1)}), bf16[1600,200]{0,1:T(8,128)(2,1)}) %reduce-scatter.38.cloned.1.call-update) | async-done | bytes 640016
  1773.9 160.0 %reduce-scatter.36.cloned.1.call-done = bf16[1600,600]{0,1:T(8,128)(2,1)} async-done(((bf16[1600,4800]{0,1:T(8,128)(2,1)}), bf16[1600,600]{0,1:T(8,128)(2,1)}) %reduce-scatter.36.cloned.1.call-update) | async-done | bytes 1920016
  1934.3 211.9 %reduce-scatter.26.cloned.1.call-done = bf16[1600,800]{0,1:T(8,128)(2,1)} async-done(((bf16[1600,6400]{0,1:T(8,128)(2,1)}), bf16[1600,800]{0,1:T(8,128)(2,1)}) %reduce-scatter.26.cloned.1.call-update) | async-done | bytes 2560016 | tf_op jit(solution)/shard_map/reduce_scatter | solution.py:202
  2149.8 43.7 %reduce-scatter.42.cloned.1.call-done = bf16[200,1600]{1,0:T(8,128)(2,1)} async-done(((bf16[800,1600]{1,0:T(8,128)(2,1)}), bf16[200,1600]{1,0:T(8,128)(2,1)}) %reduce-scatter.42.cloned.1.call-update) | async-done | bytes 640016
  2195.8 144.1 %all-gather.52.cloned.1.call-done = bf16[1600,4800]{0,1:T(8,128)(2,1)} async-done(((bf16[1600,600]{0,1:T(8,128)(2,1)}), bf16[1600,4800]{0,1:T(8,128)(2,1)}) %all-gather.52.cloned.1.call-update) | async-done | bytes 15360016 | tf_op jit(solution)/shard_map/all_gather | solution.py:62
  2352.9 26.5 %all-reduce.11 = (bf16[8,1600]{1,0:T(8,128)(2,1)S(1)}, bf16[6400]{0:T(1024)(128)(2,1)S(1)}) all-reduce(bf16[8,1600]{1,0:T(8,128)(2,1)S(1)} %stack.44, bf16[6400]{0:T(1024)(128)(2,1)S(1)} %get-tuple-element.632), channel_id=13, replica_groups=mesh['fsdp'=4,'seq'=8] {'seq'}, use_global_device_ids=true, to_apply=%region_35.36.clone | all-reduce | flops 19200 | bytes 76800
  2395.6 44.7 %all-reduce.15.cloned.1.call-done = bf16[1600,600]{0,1:T(8,128)(2,1)} async-done(((bf16[1600,600]{0,1:T(8,128)(2,1)}), bf16[1600,600]{0,1:T(8,128)(2,1)}) %all-reduce.15.cloned.1.call-update) | async-done | bytes 1920016
  2443.0 45.9 %reduce-scatter.40.cloned.1.call-done = bf16[1600,200]{0,1:T(8,128)(2,1)} async-done(((bf16[1600,800]{0,1:T(8,128)(2,1)}), bf16[1600,200]{0,1:T(8,128)(2,1)}) %reduce-scatter.40.cloned.1.call-update) | async-done | bytes 640016
  (291 shorter events, 469.0 us)
Async XLA Ops:
  7.9 188.6 %all-gather.24.cloned.1.call-start = ((), (), s32[]{:S(2)}) async-start(), calls=%async_computation.10 | async-start | bytes 17971200 | tf_op jit(solution)/shard_map/all_gather | solution.py:62
  51.6 188.5 %all-gather.32.cloned.1.call-start = ((), (), s32[]{:S(2)}) async-start(), calls=%async_computation.14 | async-start | bytes 3328000 | tf_op jit(solution)/shard_map/all_gather | solution.py:53
  52.3 229.5 %all-gather.36.cloned.1.call-start = ((), (), s32[]{:S(2)}) async-start(), calls=%async_computation.16 | async-start | bytes 3328000 | tf_op jit(solution)/shard_map/all_gather | solution.py:54
  52.9 278.9 %all-gather.26.cloned.1.call-start = ((), (), s32[]{:S(2)}) async-start(), calls=%async_computation.11 | async-start | bytes 3686400 | tf_op jit(solution)/shard_map/all_gather | solution.py:140
  205.5 159.6 %all-gather.28.cloned.1.call-start = ((), (), s32[]{:S(2)}) async-start(), calls=%async_computation.12 | async-start | bytes 3686400 | tf_op jit(solution)/shard_map/all_gather | solution.py:141
  206.9 215.4 %all-gather.30.cloned.1.call-start = ((), (), s32[]{:S(2)}) async-start(), calls=%async_computation.13 | async-start | bytes 5990400 | tf_op jit(solution)/shard_map/all_gather | solution.py:63
  223.3 387.5 %all-gather.34.cloned.1.call-start = ((), (), s32[]{:S(2)}) async-start(), calls=%async_computation.15 | async-start | bytes 23961600 | tf_op jit(solution)/shard_map/all_gather | solution.py:95
  240.1 558.8 %all-gather.38.cloned.1.call-start = ((), (), s32[]{:S(2)}) async-start(), calls=%async_computation.17 | async-start | bytes 23961600 | tf_op jit(solution)/shard_map/all_gather | solution.py:96
  281.8 570.1 %all-gather.40.cloned.1.call-start = ((), (), s32[]{:S(2)}) async-start(), calls=%async_computation.18 | async-start | bytes 3328000 | tf_op jit(solution)/shard_map/all_gather | solution.py:54
  814.3 269.4 %all-gather.42.cloned.1.call-start = ((), (), s32[]{:S(2)}) async-start(), calls=%async_computation.19 | async-start | bytes 23961600 | tf_op jit(solution)/shard_map/all_gather | solution.py:96
  851.9 419.8 %all-gather.46.cloned.1.call-start = ((), (), s32[]{:S(2)}) async-start(), calls=%async_computation.21 | async-start | bytes 23961600 | tf_op jit(solution)/shard_map/all_gather | solution.py:95
  893.8 434.4 %all-gather.48.cloned.1.call-start = ((), (), s32[]{:S(2)}) async-start(), calls=%async_computation.22 | async-start | bytes 5990400 | tf_op jit(solution)/shard_map/all_gather | solution.py:63
  908.3 509.1 %reduce-scatter.32.cloned.1.call-start = ((), (), s32[]{:S(2)}) async-start(), calls=%async_computation.28 | async-start | bytes 3833856
  1375.9 84.9 %reduce-scatter.30.cloned.1.call-start = ((), (), s32[]{:S(2)}) async-start(), calls=%async_computation.27 | async-start | bytes 3833856
  1386.1 287.0 %reduce-scatter.28.cloned.1.call-start = ((), (), s32[]{:S(2)}) async-start(), calls=%async_computation.26 | async-start | bytes 23961600 | tf_op jit(solution)/shard_map/reduce_scatter | solution.py:205
  1399.3 308.8 %all-gather.50.cloned.1.call-start = ((), (), s32[]{:S(2)}) async-start(), calls=%async_computation.23 | async-start | bytes 2560000 | tf_op jit(solution)/shard_map/all_gather | solution.py:51
  1399.9 371.7 %reduce-scatter.38.cloned.1.call-start = ((), (), s32[]{:S(2)}) async-start(), calls=%async_computation.32 | async-start | bytes 5990400
  1404.5 529.5 %reduce-scatter.36.cloned.1.call-start = ((), (), s32[]{:S(2)}) async-start(), calls=%async_computation.31 | async-start | bytes 17971200
  1475.1 671.1 %reduce-scatter.26.cloned.1.call-start = ((), (), s32[]{:S(2)}) async-start(), calls=%async_computation.25 | async-start | bytes 23961600 | tf_op jit(solution)/shard_map/reduce_scatter | solution.py:202
  1487.7 705.8 %reduce-scatter.42.cloned.1.call-start = ((), (), s32[]{:S(2)}) async-start(), calls=%async_computation.34 | async-start | bytes 3328000
  1673.1 666.8 %all-gather.52.cloned.1.call-start = ((), (), s32[]{:S(2)}) async-start(), calls=%async_computation.24 | async-start | bytes 17971200 | tf_op jit(solution)/shard_map/all_gather | solution.py:62
  1712.2 681.5 %reduce-scatter.34.cloned.1.call-start = ((), (), s32[]{:S(2)}) async-start(), calls=%async_computation.29 | async-start | bytes 1024000
  1773.9 666.4 %all-reduce.15.cloned.1.call-start = ((), (), s32[]{:S(2)}) async-start(), calls=%async_computation.30 | async-start | bytes 3993600
  1934.0 554.9 %reduce-scatter.40.cloned.1.call-start = ((), (), s32[]{:S(2)}) async-start(), calls=%async_computation.33 | async-start | bytes 3328000
  (44 other events, 2257.5 us)
Sparse Core Ops, SparseCore 0:
  9.9 37.5 all-gather.21
  51.7 144.7 all-gather.23
  198.3 41.7 all-gather.31
  241.8 39.9 all-gather.35
  283.8 40.6 all-gather.25
  326.6 38.4 all-gather.27
  367.3 54.9 all-gather.29
  423.9 186.9 all-gather.33
  612.5 186.3 all-gather.37
  813.7 38.1 all-gather.39
  853.8 39.9 all-gather.43
  895.3 188.4 all-gather.41
  1085.4 186.3 all-gather.45
  1273.3 54.9 all-gather.47
  1376.0 41.3 reduce-scatter.31
  1419.6 41.2 reduce-scatter.29
  1463.1 209.9 reduce-scatter.27
  1710.4 61.1 reduce-scatter.37
  1773.8 160.1 reduce-scatter.35
  1936.5 209.6 reduce-scatter.25
  2149.4 44.0 reduce-scatter.41
  2195.3 144.5 all-gather.51
  2371.6 68.5 all-reduce.14
  2443.1 45.7 reduce-scatter.39
  (2 shorter events, 57.7 us)
where the time goes:
time: 2500 us
  waiting for transfers between devices  2030 us (81%)
  matrix products  177 us (7%)
  blocking collectives  169 us (7%)
  local copies, waits for them, and re-layouts  74.6 us (3%)
  other arithmetic  27.8 us (1%)
    unnamed x34, waiting for transfers between devices  411 us
    all_gather x2, waiting for transfers between devices, gather_feedforward(): lax.all_gather(matrix_fc, 'seq', axis=1, tiled=True)  357 us
    all_gather x2, waiting for transfers between devices, gather_feedforward(): lax.all_gather(matrix_proj, 'seq', axis=0, tiled=True)  318 us
    all_gather x2, waiting for transfers between devices, gather_attention(): lax.all_gather(matrix_qkv, 'seq', axis=1, tiled=True)  261 us
    reduce_scatter x1, waiting for transfers between devices, per_device(): lax.psum_scatter(grad_fc_full.astype(jnp.bfloat16), 'seq', scatter_dimens...  212 us
    reduce_scatter x1, waiting for transfers between devices, per_device(): lax.psum_scatter(grad_proj_full.astype(jnp.bfloat16), 'seq', scatter_dime...  185 us
    all_gather x2, waiting for transfers between devices, gather_owned(): lax.all_gather(matrix_proj, 'fsdp', axis=0, tiled=True)  79.2 us
    all_gather x2, waiting for transfers between devices, gather_owned(): lax.all_gather(matrix_qkv, 'fsdp', axis=0, tiled=True)  74.4 us
  transfers between devices with their start and end apart: 26, of which 24 were waited for; matrix products, arithmetic and copies ran while one was open for 8% of the time, Pallas kernels for 0%

commit v1 on v0

--- a/solution.py
+++ b/solution.py
@@ -3,6 +3,8 @@
 import jax
 import jax.numpy as jnp
 from jax import lax
+from jax.experimental import pallas as pl
+from jax.experimental.pallas import tpu as pltpu
 from jax.sharding import PartitionSpec as P
 
 HEADS = 25
@@ -66,7 +68,7 @@
     )
 
 
-def per_device(
+def gathered_weights(
     tokens,
     segment_ids,
     cotangent,
@@ -316,6 +318,807 @@
     return (result[None], input_grad[None], own_qkv, own_attn, own_fc, own_proj, own_vec, own_bias)
 
 
+resident_most = 2 * 1024 * 1024
+
+
+def contract_last(left, right):
+    return lax.dot_general(left, right, (((1,), (1,)), ((), ())), preferred_element_type=jnp.float32)
+
+
+def contract_first(left, right):
+    return lax.dot_general(left, right, (((0,), (0,)), ((), ())), preferred_element_type=jnp.float32)
+
+
+def head_lanes(head, shape):
+    lane = lax.broadcasted_iota(jnp.int32, shape, 1)
+    return (lane >= head * HEAD_DIM) & (lane < (head + 1) * HEAD_DIM)
+
+
+def only_head(values, head):
+    return jnp.where(head_lanes(head, values.shape), values, jnp.zeros_like(values))
+
+
+def tile_pairs(length, tile, reach):
+    for start in range(0, length, tile):
+        first = max(0, (start - reach) // tile * tile)
+        yield start, first, start + tile - first
+
+
+def allowed_pairs(ids_col, ids_row, start, first, tile, count):
+    q_pos = start + lax.broadcasted_iota(jnp.int32, (tile, count), 0)
+    k_pos = first + lax.broadcasted_iota(jnp.int32, (tile, count), 1)
+    return (k_pos <= q_pos) & (ids_col[start : start + tile, :1] == ids_row[:1, first : first + count])
+
+
+def attention_backward_kernel(
+    tile, reach, qkv_ref, attn_ref, grad_ref, lse_ref, ids_col, ids_row, out_ref
+):
+    head = pl.program_id(0)
+    length, span = attn_ref.shape
+    scale = HEAD_DIM**-0.5
+
+    @pl.when(head == 0)
+    def _():
+        out_ref[...] = jnp.zeros_like(out_ref)
+
+    for start, first, count in tile_pairs(length, tile, reach):
+        rows, keys = pl.ds(start, tile), pl.ds(first, count)
+        query = only_head(qkv_ref[rows, :span], head)
+        key = qkv_ref[keys, span : 2 * span]
+        grad = only_head(grad_ref[rows, :], head)
+        delta = jnp.sum(
+            grad.astype(jnp.float32) * attn_ref[rows, :].astype(jnp.float32), axis=1, keepdims=True
+        )
+        scores = contract_last(query, key) * scale
+        allowed = allowed_pairs(ids_col, ids_row, start, first, tile, count)
+        probs = jnp.where(allowed, jnp.exp(scores - lse_ref[0, rows, :]), 0.0)
+        prob_grad = contract_last(grad, qkv_ref[keys, 2 * span :])
+        score_grad = (probs * (prob_grad - delta)).astype(jnp.bfloat16)
+        out_ref[rows, :span] += scale * jnp.dot(
+            score_grad, only_head(key, head), preferred_element_type=jnp.float32
+        )
+        out_ref[keys, span : 2 * span] += scale * contract_first(score_grad, query)
+        out_ref[keys, 2 * span :] += contract_first(probs.astype(jnp.bfloat16), grad)
+
+
+def whole(shape):
+    return pl.BlockSpec(shape, lambda head: (0,) * len(shape))
+
+
+def per_head(shape):
+    return pl.BlockSpec((1,) + shape, lambda head: (head,) + (0,) * len(shape))
+
+
+def attention_backward(qkv, attn, grad, lse, ids_col, ids_row, reach):
+    length, span = attn.shape
+    tile = min(256, length)
+    return pl.pallas_call(
+        lambda *refs: attention_backward_kernel(tile, reach, *refs),
+        grid=(lse.shape[0],),
+        in_specs=[
+            whole(qkv.shape),
+            whole(attn.shape),
+            whole(grad.shape),
+            per_head((length, 1)),
+            whole(ids_col.shape),
+            whole(ids_row.shape),
+        ],
+        out_specs=whole(qkv.shape),
+        out_shape=jax.ShapeDtypeStruct(qkv.shape, jnp.float32),
+        compiler_params=pltpu.CompilerParams(vmem_limit_bytes=48 * 1024 * 1024),
+    )(qkv, attn, grad, lse, ids_col, ids_row)
+
+
+def join_seq(block, axis=0):
+    return lax.all_gather(block, "seq", axis=axis, tiled=True)
+
+
+def join_fsdp(block, axis=0):
+    return lax.all_gather(block, "fsdp", axis=axis, tiled=True)
+
+
+def sum_seq(terms, axis=0):
+    return lax.psum_scatter(
+        terms.astype(jnp.bfloat16), "seq", scatter_dimension=axis, tiled=True
+    ).astype(jnp.float32)
+
+
+def sum_fsdp(terms, axis=0):
+    return lax.psum_scatter(
+        terms.astype(jnp.bfloat16), "fsdp", scatter_dimension=axis, tiled=True
+    ).astype(jnp.float32)
+
+
+MESH = pl.DeviceIdType.MESH
+
+
+def remote(source, target, sent, landed, axis, index):
+    return pltpu.make_async_remote_copy(
+        src_ref=source,
+        dst_ref=target,
+        send_sem=sent,
+        recv_sem=landed,
+        device_id={axis: index},
+        device_id_type=MESH,
+    )
+
+
+def greet(row, plane):
+    barrier = pltpu.get_barrier_semaphore()
+    for axis, size in (("seq", row), ("fsdp", plane)):
+        own = lax.axis_index(axis)
+        for ahead in range(1, size):
+            pl.semaphore_signal(
+                barrier,
+                inc=1,
+                device_id={axis: lax.rem(own + ahead, size)},
+                device_id_type=MESH,
+            )
+    pl.semaphore_wait(barrier, row + plane - 2)
+
+
+class RowGather:
+    def __init__(self, own, view, sent, landed, row, chunks=1, has=None):
+        self.own, self.view, self.sent, self.landed = own, view, sent, landed
+        self.row, self.chips, self.chunks = row, row // 2, chunks
+        self.has = has or (lambda i, c: None)
+        self.me = lax.axis_index("seq")
+        self.chip, self.core = self.me // 2, self.me % 2
+        self.other = self.me + 1 - 2 * self.core
+
+    def hop(self, i, c, way, source=None):
+        place = self.view(i, c)
+        target = (self.me + 2, self.me - 2, self.other)[way]
+        return remote(
+            place if source is None else source,
+            place,
+            self.sent.at[i, c, way],
+            self.landed.at[i, c],
+            "seq",
+            target,
+        )
+
+    def when(self, i, c, condition, action):
+        has = self.has(i, c)
+        if has is not None:
+            condition = has if condition is None else has & condition
+        if condition is None:
+            action()
+        else:
+            pl.when(condition)(action)
+
+    def spread(self, i, c, forward, backward, source=None):
+        self.when(i, c, forward, lambda: self.hop(i, c, 0, source).start())
+        self.when(i, c, backward, lambda: self.hop(i, c, 1, source).start())
+        self.when(i, c, None, lambda: self.hop(i, c, 2, source).start())
+
+    def start(self):
+        for c in range(self.chunks):
+            self.spread(
+                self.me, c, self.chip < self.chips - 1, self.chip > 0, self.own(c) if self.own else None
+            )
+
+    def pass_on(self, distance):
+        def from_before():
+            i = self.me - 2 * distance
+            for c in range(self.chunks):
+                self.when(i, c, None, lambda: self.hop(i, c, 2).wait_recv())
+                self.when(i, c, self.chip < self.chips - 1, lambda: self.hop(i, c, 0).start())
+                self.when(i, c, None, lambda: self.hop(i, c, 2).start())
+
+        def from_after():
+            i = self.me + 2 * distance
+            for c in range(self.chunks):
+                self.when(i, c, None, lambda: self.hop(i, c, 2).wait_recv())
+                self.when(i, c, self.chip > 0, lambda: self.hop(i, c, 1).start())
+                self.when(i, c, None, lambda: self.hop(i, c, 2).start())
+
+        pl.when(self.chip >= distance)(from_before)
+        pl.when(self.chip + distance < self.chips)(from_after)
+
+    def from_other_core(self):
+        for k in range(self.chips):
+            i = 2 * k + 1 - self.core
+            for c in range(self.chunks):
+                self.when(i, c, None, lambda: self.hop(i, c, 2).wait_recv())
+
+    def drain(self):
+        for k in range(self.chips):
+            i = 2 * k + self.core
+            for c in range(self.chunks):
+                forward = (self.chip >= k) & (self.chip < self.chips - 1)
+                backward = (self.chip <= k) & (self.chip > 0)
+                self.when(i, c, forward, lambda: self.hop(i, c, 0).wait_send())
+                self.when(i, c, backward, lambda: self.hop(i, c, 1).wait_send())
+                self.when(i, c, None, lambda: self.hop(i, c, 2).wait_send())
+
+
+class PlaneGather:
+    def __init__(self, own, view, parts, sent, landed):
+        self.own, self.view, self.parts, self.sent, self.landed = own, view, parts, sent, landed
+        me = lax.axis_index("fsdp")
+        self.me = me
+        self.beside = me + 1 - 2 * (me % 2)
+        self.above = lax.rem(me + 2, 4)
+        self.corner = lax.rem(self.beside + 2, 4)
+
+    def whole(self, i, slot, target, source=None):
+        place = self.view(i, None)
+        return remote(
+            place if source is None else source,
+            place,
+            self.sent.at[slot],
+            self.landed.at[slot],
+            "fsdp",
+            target,
+        )
+
+    def part(self, i, slot, target):
+        place = self.view(i, self.parts[slot - 2])
+        return remote(place, place, self.sent.at[slot], self.landed.at[slot], "fsdp", target)
+
+    def start(self):
+        self.whole(self.me, 0, self.beside, self.own).start()
+        self.whole(self.me, 1, self.above, self.own).start()
+
+    def pass_on(self):
+        self.whole(self.beside, 0, self.beside).wait_recv()
+        self.part(self.beside, 2, self.above).start()
+        self.whole(self.above, 1, self.above).wait_recv()
+        self.part(self.above, 3, self.beside).start()
+
+    def finish(self):
+        self.part(self.corner, 2, self.above).wait_recv()
+        self.part(self.corner, 3, self.beside).wait_recv()
+
+    def drain(self):
+        self.whole(self.me, 0, self.beside).wait_send()
+        self.whole(self.me, 1, self.above).wait_send()
+        self.part(self.beside, 2, self.above).wait_send()
+        self.part(self.above, 3, self.beside).wait_send()
+
+
+def group_of(device):
+    third = (device + 5) // 8 - (device + 4) // 8
+    fifth = (device + 3) // 8 - (device + 2) // 8
+    return device - (device + 4) // 8 - (device + 2) // 8 + 3 * third + 3 * fifth
+
+
+def device_of(group):
+    return group + (group + 5) // 8 + (group + 4) // 8 - 5 * ((group + 2) // 8)
+
+
+def own_blocks(device, columns, width, span):
+    groups = -(-width // span)
+
+    def block_at(column):
+        return groups * (column // width) + (column % width) // span
+
+    return block_at(device * columns), block_at(device * columns + columns - 1)
+
+
+def norm_rows(values, gain, shift):
+    centred = values - jnp.mean(values, axis=-1, keepdims=True)
+    inverse = lax.rsqrt(jnp.mean(centred * centred, axis=-1, keepdims=True) + norm_eps)
+    return (centred * inverse) * gain + shift
+
+
+def attend(head, start, first, count, tile, qkv_ref, ids_col, ids_row, out_ref, lse_ref):
+    span = out_ref.shape[1]
+    rows, keys = pl.ds(start, tile), pl.ds(first, count)
+    query = only_head(qkv_ref[rows, :span], head)
+    scores = contract_last(query, qkv_ref[keys, span : 2 * span]) * (HEAD_DIM**-0.5)
+    q_pos = start + lax.broadcasted_iota(jnp.int32, (tile, count), 0)
+    k_pos = first + lax.broadcasted_iota(jnp.int32, (tile, count), 1)
+    allowed = (k_pos <= q_pos) & (ids_col[rows, :1] == ids_row[:1, keys])
+    masked = jnp.where(allowed, scores, masked_score)
+    top = jnp.max(masked, axis=1, keepdims=True)
+    weights = jnp.exp(masked - top)
+    total = jnp.sum(weights, axis=1, keepdims=True)
+    probs = (weights * (1.0 / total)).astype(jnp.bfloat16)
+    value = only_head(qkv_ref[keys, 2 * span :], head)
+    mixed = jnp.dot(probs, value, preferred_element_type=jnp.float32)
+    out_ref[rows, :] += mixed.astype(jnp.bfloat16)
+    lse_ref[head, rows, :] = top + jnp.log(total)
+
+
+def attention_kernel(
+    reach,
+    x_ref,
+    cot_ref,
+    small_ref,
+    blocks_ref,
+    fc_ref,
+    proj_ref,
+    x_all,
+    cot_all,
+    small_all,
+    h1_all,
+    qkv_all,
+    w_all,
+    lse_all,
+    attn_own_out,
+    attn_all,
+    fc_all,
+    proj_all,
+    x_v,
+    small_v,
+    vec,
+    ids_col,
+    ids_row,
+    pieces,
+    w_v,
+    h1_v,
+    qkv_v,
+    attn_v,
+    small_sent,
+    small_landed,
+    plane_sent,
+    plane_landed,
+    piece_sent,
+    piece_landed,
+    w_sent,
+    w_landed,
+    x_sent,
+    x_landed,
+    cot_sent,
+    cot_landed,
+    attn_sent,
+    attn_landed,
+    fc_sent,
+    fc_landed,
+    proj_sent,
+    proj_landed,
+    local_sem,
+):
+    row, plane = 8, 4
+    seq, fsdp = lax.axis_index("seq"), lax.axis_index("fsdp")
+    own_rows, width = x_ref.shape
+    span = attn_v.shape[1]
+    length = own_rows * row
+    depth = blocks_ref.shape[1]
+    groups = -(-width // span)
+    group = group_of(seq)
+    used = []
+
+    def keep(source, target):
+        copy = pltpu.make_async_copy(source, target, local_sem.at[len(used)])
+        copy.start()
+        used.append(copy)
+
+    vec[...] = jnp.zeros_like(vec)
+    w_v[...] = jnp.zeros_like(w_v)
+    greet(row, plane)
+    own_small = pltpu.make_async_copy(small_ref, small_v.at[fsdp, seq], small_landed.at[seq])
+    own_small.start()
+
+    def small_to(target, slot):
+        return remote(
+            small_ref, small_v.at[fsdp, seq], small_sent.at[slot], small_landed.at[seq], "seq", target
+        )
+
+    for ahead in range(1, row):
+        small_to(lax.rem(seq + ahead, row), ahead - 1).start()
+
+    first_block, last_block = own_blocks(seq, qkv_columns(width, row), width, span)
+
+    def piece(k):
+        block = first_block + k
+        kind, at = block // groups, block % groups
+        begins = kind * width + at * span
+        later = (seq * qkv_columns(width, row) + width * 3 - begins - 1) // (width * 3)
+        target = device_of(at)
+        place = pieces.at[kind, later]
+        return block <= last_block, target, place, piece_landed.at[kind, later]
+
+    for k in range(4):
+        there, target, place, landed = piece(k)
+
+        @pl.when(there & (target == seq))
+        def _():
+            pltpu.make_async_copy(blocks_ref.at[k], place, landed).start()
+
+        @pl.when(there & (target != seq))
+        def _():
+            remote(blocks_ref.at[k], place, piece_sent.at[k], landed, "seq", target).start()
+
+    x_line = RowGather(lambda c: x_ref, lambda i, c: x_v.at[i], x_sent, x_landed, row)
+    own_x = pltpu.make_async_copy(x_ref, x_v.at[seq], local_sem.at[0])
+    own_x.start()
+    used.append(None)
+    x_line.start()
+
+    for other in range(row):
+        pltpu.make_async_copy(small_ref, small_v.at[fsdp, other], small_landed.at[other]).wait()
+
+    def small_plane(ahead):
+        return remote(
+            small_v.at[fsdp],
+            small_v.at[fsdp],
+            plane_sent.at[ahead - 1],
+            plane_landed.at[ahead - 1],
+            "fsdp",
+            lax.rem(fsdp + ahead, plane),
+        )
+
+    for ahead in range(1, plane):
+        small_plane(ahead).start()
+    for other in range(row):
+        lanes = pl.ds(other * own_rows, own_rows)
+        ids = jnp.broadcast_to(small_v[fsdp, other, 3:4, :own_rows], (own_rows, own_rows))
+        ids_row[:, lanes] = ids[:8]
+        ids_col[lanes, :] = ids.T
+    for ahead in range(1, plane):
+        remote(
+            small_v.at[fsdp],
+            small_v.at[lax.rem(fsdp + plane - ahead, plane)],
+            plane_sent.at[ahead - 1],
+            plane_landed.at[ahead - 1],
+            "fsdp",
+            lax.rem(fsdp + ahead, plane),
+        ).wait_recv()
+    share = width // row
+    for i in range(plane):
+        for other in range(row):
+            vec[2 * i : 2 * i + 2, share * other : share * (other + 1)] = small_v[i, other, 0:2, :share]
+
+    own_w = pl.ds(pl.multiple_of(fsdp * depth, 16), depth)
+
+    @pl.when(group < groups)
+    def _():
+        for kind in range(3):
+            begins = kind * width + group * span
+            ends = begins + jnp.minimum(span, width - group * span) - 1
+            cols = qkv_columns(width, row)
+            straddles = ends // cols != begins // cols
+            pltpu.make_async_copy(
+                blocks_ref.at[0], pieces.at[kind, 0], piece_landed.at[kind, 0]
+            ).wait()
+            w_v[own_w, kind * span : (kind + 1) * span] = pieces[kind, 0]
+
+            @pl.when(straddles)
+            def _():
+                pltpu.make_async_copy(
+                    blocks_ref.at[0], pieces.at[kind, 1], piece_landed.at[kind, 1]
+                ).wait()
+                w_v[own_w, kind * span : (kind + 1) * span] = pieces[kind, 0] + pieces[kind, 1]
+
+    def w_view(i, part):
+        start, count = (0, depth) if part is None else part
+        return w_v.at[pl.ds(pl.multiple_of(i * depth + start, 16), count)]
+
+    half = depth // 32 * 16
+    w_plane = PlaneGather(None, w_view, ((0, half), (half, depth - half)), w_sent, w_landed)
+    w_plane.start()
+    x_line.pass_on(1)
+    w_plane.pass_on()
+
+    def slab(target):
+        def view(i, part):
+            start, count = (0, target.shape[1]) if part is None else part
+            return target.at[i, pl.ds(start, count)]
+
+        return view
+
+    units = fc_ref.shape[0]
+    cut = units // 32 * 16
+    parts = ((0, cut), (cut, units - cut))
+    fc_plane = PlaneGather(fc_ref, slab(fc_all), parts, fc_sent, fc_landed)
+    proj_plane = PlaneGather(proj_ref, slab(proj_all), parts, proj_sent, proj_landed)
+    fc_plane.start()
+    proj_plane.start()
+    x_line.pass_on(2)
+    x_line.pass_on(3)
+    cot_line = RowGather(lambda c: cot_ref, lambda i, c: cot_all.at[i], cot_sent, cot_landed, row)
+    cot_line.start()
+    keep(cot_ref, cot_all.at[seq])
+    keep(fc_ref, fc_all.at[fsdp])
+    keep(proj_ref, proj_all.at[fsdp])
+    x_line.from_other_core()
+    own_x.wait()
+    w_plane.finish()
+    lanes = pl.ds(pl.multiple_of(group * span, span), span)
+    query_shift, value_shift = vec[2:3, lanes], vec[3:4, lanes]
+
+    def project(i, carry):
+        hidden = norm_rows(x_v[i].astype(jnp.float32), vec[0:1, :width], vec[1:2, :width])
+        hidden = hidden.astype(jnp.bfloat16)
+        h1_v[i] = hidden
+        rows = pl.ds(pl.multiple_of(i * own_rows, own_rows), own_rows)
+        mixed = jnp.dot(hidden, w_v[...], preferred_element_type=jnp.float32)
+        qkv_v[rows, :span] = (mixed[:, :span] + query_shift).astype(jnp.bfloat16)
+        qkv_v[rows, span : 2 * span] = mixed[:, span : 2 * span].astype(jnp.bfloat16)
+        qkv_v[rows, 2 * span :] = (mixed[:, 2 * span :] + value_shift).astype(jnp.bfloat16)
+        return carry
+
+    lax.fori_loop(0, row, project, 0)
+    cot_line.pass_on(1)
+    keep(x_v, x_all)
+    keep(small_v, small_all)
+    keep(h1_v, h1_all)
+    keep(qkv_v, qkv_all)
+    keep(w_v, w_all)
+
+    attn_v[...] = jnp.zeros_like(attn_v)
+    tile = 256
+
+    def heads(h, carry):
+        for start, first, count in tile_pairs(length, tile, reach):
+            attend(h, start, first, count, tile, qkv_v, ids_col, ids_row, attn_v, lse_all)
+        return carry
+
+    lax.fori_loop(0, 2, heads, 0)
+    cot_line.pass_on(2)
+    lax.fori_loop(2, 4, heads, 0)
+
+    def chunk(i, c):
+        return attn_all.at[:, pl.ds(pl.multiple_of(group_of(i) * span + c * 128, 128), 128)]
+
+    attn_line = RowGather(
+        lambda c: attn_v.at[:, pl.ds(c * 128, 128)],
+        chunk,
+        attn_sent,
+        attn_landed,
+        row,
+        chunks=2,
+        has=lambda i, c: group_of(i) < groups - c,
+    )
+    attn_line.start()
+    for c in range(2):
+        lanes = pl.ds(pl.multiple_of(group * span + c * 128, 128), 128)
+
+        @pl.when(group < groups - c)
+        def _():
+            pltpu.make_async_copy(
+                attn_v.at[:, pl.ds(c * 128, 128)], attn_all.at[:, lanes], piece_landed.at[c, 0]
+            ).start()
+
+    keep(attn_v, attn_own_out)
+    fc_plane.pass_on()
+    proj_plane.pass_on()
+    cot_line.pass_on(3)
+    for distance in range(1, row // 2):
+        attn_line.pass_on(distance)
+    attn_line.from_other_core()
+    cot_line.from_other_core()
+    fc_plane.finish()
+    proj_plane.finish()
+
+    for c in range(2):
+        lanes = pl.ds(pl.multiple_of(group * span + c * 128, 128), 128)
+
+        @pl.when(group < groups - c)
+        def _():
+            pltpu.make_async_copy(
+                attn_v.at[:, pl.ds(c * 128, 128)], attn_all.at[:, lanes], piece_landed.at[c, 0]
+            ).wait()
+
+    for ahead in range(1, row):
+        small_to(lax.rem(seq + ahead, row), ahead - 1).wait_send()
+    for ahead in range(1, plane):
+        small_plane(ahead).wait_send()
+    for k in range(4):
+        there, target, place, landed = piece(k)
+
+        @pl.when(there & (target != seq))
+        def _():
+            remote(blocks_ref.at[k], place, piece_sent.at[k], landed, "seq", target).wait_send()
+
+    for line in (x_line, cot_line, attn_line, w_plane, fc_plane, proj_plane):
+        line.drain()
+    for copy in used:
+        if copy is not None:
+            copy.wait()
+
+
+def qkv_columns(width, row):
+    return 3 * width // row
+
+
+def attention_phase(x_own, cot_own, small, blocks, fc_own, proj_own, reach):
+    own_rows, width = x_own.shape
+    row, plane, span = 8, 4, 256
+    length = own_rows * row
+    units = fc_own.shape[0]
+    bf, f32 = jnp.bfloat16, jnp.float32
+    anywhere = pl.BlockSpec(memory_space=pl.ANY)
+    in_vmem = pl.BlockSpec(memory_space=pltpu.VMEM)
+    dma = pltpu.SemaphoreType.DMA
+
+    def shaped(*shape, dtype=bf):
+        return jax.ShapeDtypeStruct(shape, dtype)
+
+    return pl.pallas_call(
+        lambda *refs: attention_kernel(reach, *refs),
+        out_shape=[
+            shaped(row, own_rows, width),
+            shaped(row, own_rows, width),
+            shaped(plane, row, 8, span, dtype=f32),
+            shaped(row, own_rows, width),
+            shaped(length, 3 * span),
+            shaped(width, 3 * span),
+            shaped(4, length, 1, dtype=f32),
+            shaped(length, span),
+            shaped(length, 7 * span),
+            shaped(plane, units, width),
+            shaped(plane, units, width),
+        ],
+        in_specs=[anywhere] * 6,
+        out_specs=[anywhere] * 6 + [in_vmem] + [anywhere] * 4,
+        scratch_shapes=[
+            pltpu.VMEM((row, own_rows, width), bf),
+            pltpu.VMEM((plane, row, 8, span), f32),
+            pltpu.VMEM((8, 8 * span), f32),
+            pltpu.VMEM((length, own_rows), f32),
+            pltpu.VMEM((8, length), f32),
+            pltpu.VMEM((3, 2, width // plane, span), bf),
+            pltpu.VMEM((width, 3 * span), bf),
+            pltpu.VMEM((row, own_rows, width), bf),
+            pltpu.VMEM((length, 3 * span), bf),
+            pltpu.VMEM((length, span), bf),
+            dma((row - 1,)),
+            dma((row,)),
+            dma((plane - 1,)),
+            dma((plane - 1,)),
+            dma((4,)),
+            dma((3, 2)),
+            dma((4,)),
+            dma((4,)),
+            dma((row, 1, 3)),
+            dma((row, 1)),
+            dma((row, 1, 3)),
+            dma((row, 1)),
+            dma((row, 2, 3)),
+            dma((row, 2)),
+            dma((4,)),
+            dma((4,)),
+            dma((4,)),
+            dma((4,)),
+            dma((12,)),
+        ],
+        compiler_params=pltpu.CompilerParams(
+            collective_id=0, has_side_effects=True, vmem_limit_bytes=50 * 1024 * 1024
+        ),
+    )(x_own, cot_own, small, blocks, fc_own, proj_own)
+
+
+def column_blocks(shard, own, width, span):
+    columns = shard.shape[1]
+    groups = -(-width // span)
+    first, last = own_blocks(own, columns, width, span)
+    place = lax.iota(jnp.int32, 4 * span)
+    block, lane = first + place // span, place % span
+    at = (block % groups) * span + lane
+    there = (block <= last) & (at < width)
+    source = jnp.where(there, (block // groups) * width + at - own * columns, -1)
+    chosen = lax.broadcasted_iota(jnp.int32, (columns, 4 * span), 0) == source[None, :]
+    cut = jnp.dot(shard, chosen.astype(jnp.bfloat16), preferred_element_type=jnp.float32)
+    return cut.astype(jnp.bfloat16).reshape(-1, 4, span).transpose(1, 0, 2)
+
+
+def token_plan(
+    tokens,
+    segment_ids,
+    cotangent,
+    qkv_weight,
+    attn_out_weight,
+    fc_weight,
+    proj_weight,
+    vectors,
+    fc_bias,
+):
+    own_rows, width = tokens.shape[1], tokens.shape[2]
+    parts = lax.axis_size("seq")
+    own = lax.axis_index("seq")
+    length = own_rows * parts
+    reach = length // 2
+    span = 4 * HEAD_DIM
+    share = vectors.shape[1]
+    units = proj_weight.shape[0]
+    extra = -units % 16
+    group = group_of(own)
+
+    lines = [vectors.astype(jnp.float32), fc_bias.astype(jnp.float32)[None]]
+    lines = [jnp.pad(line, ((0, 0), (0, span - share))) for line in lines]
+    lines.append(jnp.pad(segment_ids.astype(jnp.float32), ((0, 4), (0, span - own_rows))))
+    small = jnp.concatenate(lines)
+    blocks = column_blocks(qkv_weight, own, width, span)
+    fc_own = jnp.pad(fc_weight.T, ((0, extra), (0, 0)))
+    proj_own = jnp.pad(proj_weight, ((0, extra), (0, 0)))
+    w_attn = join_fsdp(join_seq(attn_out_weight, 1))
+
+    inputs_all, grad_out_all, small_all, hidden1, qkv, w_qkv, lse, attn_own, attn_all, w_fc, w_proj = (
+        attention_phase(tokens[0], cotangent[0], small, blocks, fc_own, proj_own, reach)
+    )
+    inputs_all = inputs_all.reshape(length, width)
+    grad_out_all = grad_out_all.reshape(length, width)
+    hidden1 = hidden1.reshape(length, width)
+    w_fc, w_proj = w_fc.reshape(-1, width), w_proj.reshape(-1, width)
+    vector_rows = small_all[:, :, :2, :share].transpose(0, 2, 1, 3).reshape(-1, width)
+    own_small = lax.dynamic_index_in_dim(small_all, own, 1, keepdims=False)
+    fc_shift = jnp.pad(own_small[:, 2, :units], ((0, 0), (0, extra))).reshape(-1)
+    ids_all = lax.dynamic_index_in_dim(small_all, lax.axis_index("fsdp"), 0, keepdims=False)
+    ids_all = ids_all[:, 3, :own_rows].reshape(length)
+    ids_col, ids_row = ids_all[:, None], ids_all[None, :]
+    attn_bf = attn_all[:, :width]
+
+    def own_tokens(values):
+        return lax.dynamic_slice_in_dim(values, own * own_rows, own_rows)
+
+    resid = (
+        inputs_all.astype(jnp.float32)
+        + jnp.dot(attn_bf, w_attn, preferred_element_type=jnp.float32)
+        + vector_rows[4]
+    )
+
+    normed2, inverse2, shifted2 = layer_norm(resid, vector_rows[5], vector_rows[6])
+    hidden2 = shifted2.astype(jnp.bfloat16)
+    preact = contract_last(hidden2, w_fc) + fc_shift
+    gelu_value, gelu_slope = gelu_parts(preact)
+    act_bf = gelu_value.astype(jnp.bfloat16)
+    grad_act = contract_last(grad_out_all, w_proj)
+    grad_pre = grad_act * gelu_slope
+    grad_pre_bf = grad_pre.astype(jnp.bfloat16)
+    grad_hidden2 = sum_seq(jnp.dot(grad_pre_bf, w_fc, preferred_element_type=jnp.float32))
+    result = (
+        own_tokens(resid)
+        + sum_seq(jnp.dot(act_bf, w_proj, preferred_element_type=jnp.float32))
+        + vector_rows[7]
+    )
+    own_proj = sum_fsdp(contract_first(act_bf, grad_out_all))[:units]
+    own_fc = sum_fsdp(contract_first(grad_pre_bf, hidden2))[:units].T
+    own_bias = sum_fsdp(jnp.sum(grad_pre, axis=0))[:units]
+
+    grad_out = cotangent[0].astype(jnp.float32)
+    grad_resid_norm, gain2_grad, shift2_grad = norm_back(
+        grad_hidden2, own_tokens(normed2), own_tokens(inverse2), vector_rows[5]
+    )
+    grad_resid = grad_out + grad_resid_norm
+    grad_resid_all = join_seq(grad_resid.astype(jnp.bfloat16))
+    padded_rows = jnp.pad(w_attn, ((0, 8 * span - width), (0, 0)))
+    attn_rows = lax.dynamic_slice_in_dim(padded_rows, group * span, span)
+    grad_attn = contract_last(grad_resid_all, attn_rows).astype(jnp.bfloat16)
+    grad_qkv = attention_backward(qkv, attn_own, grad_attn, lse, ids_col, ids_row, reach)
+    grad_qkv_bf = grad_qkv.astype(jnp.bfloat16)
+    grad_hidden1 = sum_seq(contract_last(grad_qkv_bf, w_qkv))
+    normed1, inverse1, _ = layer_norm(tokens[0].astype(jnp.float32), vector_rows[0], vector_rows[1])
+    grad_input_norm, gain1_grad, shift1_grad = norm_back(
+        grad_hidden1, normed1, inverse1, vector_rows[0]
+    )
+    input_grad = grad_resid + grad_input_norm
+
+    out_columns = attn_out_weight.shape[1]
+    own_columns = lax.dynamic_slice_in_dim(grad_resid_all, own * out_columns, out_columns, axis=1)
+    own_attn = sum_fsdp(contract_first(attn_bf, own_columns))
+    qkv_terms = sum_fsdp(contract_first(hidden1, grad_qkv_bf)).astype(jnp.bfloat16)
+    spread = lax.all_gather(qkv_terms, "seq", axis=0).reshape(parts, -1, 3, span)
+    natural = jnp.concatenate(
+        [spread[i] for i in (0, 1, 2, 4, 6, 7)] + [spread[3, :, :, : width % span]], axis=2
+    ).reshape(-1, 3 * width)
+    columns = qkv_weight.shape[1]
+    own_qkv = lax.dynamic_slice_in_dim(natural, own * columns, columns, axis=1).astype(jnp.float32)
+
+    def at_own_lanes(sums):
+        padded = jnp.zeros((8 * span,), jnp.float32)
+        return lax.dynamic_update_slice_in_dim(padded, sums, group * span, 0)[:width]
+
+    column_sums = jnp.sum(grad_qkv, axis=0)
+    vector_grad = jnp.stack(
+        [
+            gain1_grad,
+            shift1_grad,
+            at_own_lanes(column_sums[:span]),
+            at_own_lanes(column_sums[2 * span :]),
+            jnp.sum(grad_resid, axis=0),
+            gain2_grad,
+            shift2_grad,
+            jnp.sum(grad_out, axis=0),
+        ]
+    )
+    own_vec = sum_fsdp(sum_seq(vector_grad, 1))
+    return (result[None], input_grad[None], own_qkv, own_attn, own_fc, own_proj, own_vec, own_bias)
+
+
 def solution(mesh):
     in_specs = (
         P("fsdp", "seq", None),
@@ -338,6 +1141,14 @@
         P("fsdp", "seq"),
         P(("fsdp", "seq")),
     )
+
+    def per_device(tokens, *rest):
+        length = tokens.shape[1] * mesh.shape["seq"]
+        fits = length * tokens.shape[2] <= resident_most
+        square = mesh.shape["fsdp"] == 4 and mesh.shape["seq"] == 8
+        plan = token_plan if fits and square else gathered_weights
+        return plan(tokens, *rest)
+
     return jax.shard_map(
         per_device, mesh=mesh, in_specs=in_specs, out_specs=out_specs, check_vma=False
     )

time: 2500 us -> 725 us (0.29)
  waiting for transfers between devices: 2030 us -> 343 us
  Pallas kernels: 0 us -> 138 us
  blocking collectives: 169 us -> 37.9 us
  matrix products: 177 us -> 71.2 us
    all_gather x16 -> x4, waiting for transfers between devices: 1220 us -> 76.7 us  [the longest x2 67.3 us: join_seq(): return lax.all_gather(block, 'seq', axis=axis, tiled=True)]
    unnamed x34 -> x11, waiting for transfers between devices: 411 us -> 115 us
    reduce_scatter x2 -> x5, waiting for transfers between devices: 397 us -> 152 us  [the longest x3 128 us: sum_seq(): lax.psum_scatter(terms.astype(jnp.bfloat16), 'seq', scatter_dimension=axi...]
    pallas_call x0 -> x2, Pallas kernels: none -> 138 us  [the longest x1 127 us: attention_phase(): pl.pallas_call(lambda *refs: attention_kernel(reach, *refs), out_shape=[s...]
    dot_general x26 -> x12, matrix products: 177 us -> 71.2 us  [the longest x4 27 us: contract_first(): lax.dot_general(left, right, (((0,), (0,)), ((), ())), preferred_element_...]
    all_gather x7 -> x0, blocking collectives: 96 us -> none  [the longest x2 41 us: gather_attention(): lax.all_gather(vector_part, 'seq', axis=1, tiled=True)]
    unnamed x4 -> x2, blocking collectives: 72.7 us -> 37.9 us
  transfers between devices with their start and end apart: 26 -> 10, of which waited for: 24 -> 8; matrix products, arithmetic and copies ran while one was open for 8% -> 10% of each run, Pallas kernels for 0% -> 18%
where the time goes in v1:
time: 725 us; the launch traced here: 717 us
  waiting for transfers between devices  343 us (47%)
  Pallas kernels  138 us (19%)
  local copies, waits for them, and re-layouts  86.5 us (12%)
  matrix products  71.2 us (10%)
  blocking collectives  37.9 us (5%)
  other arithmetic  21.8 us (3%)
  between operations  17.3 us (2%)
    reduce_scatter x3, waiting for transfers between devices, sum_seq(): lax.psum_scatter(terms.astype(jnp.bfloat16), 'seq', scatter_dimension=axi...  128 us
    pallas_call x1, Pallas kernels, attention_phase(): pl.pallas_call(lambda *refs: attention_kernel(reach, *refs), out_shape=[s...  127 us
    unnamed x11, waiting for transfers between devices  115 us
    all_gather x2, waiting for transfers between devices, join_seq(): return lax.all_gather(block, 'seq', axis=axis, tiled=True)  67.3 us
    unnamed x2, blocking collectives  37.9 us
    dot_general x4, matrix products, contract_first(): lax.dot_general(left, right, (((0,), (0,)), ((), ())), preferred_element_...  27 us
    unnamed x72, local copies, waits for them, and re-layouts  23.9 us
    reduce_scatter x2, waiting for transfers between devices, sum_fsdp(): lax.psum_scatter(terms.astype(jnp.bfloat16), 'fsdp', scatter_dimension=ax...  23.4 us
  transfers between devices with their start and end apart: 10, of which 8 were waited for; matrix products, arithmetic and copies ran while one was open for 10% of the time, Pallas kernels for 18%

profile of v1, /device:TPU:0, one launch (start us, length us, event | category | flops | bytes accessed | tf_op | source)
XLA Modules:
  0.0 717.2 jit_solution(16145713145030731894)
XLA Ops:
  9.2 29.2 %all-gather.6.cloned.1.call-done = bf16[400,1600]{0,1:T(8,128)(2,1)} async-done(((bf16[400,200]{0,1:T(8,128)(2,1)}), bf16[400,1600]{0,1:T(8,128)(2,1)}) %all-gather.6.cloned.1.call-update) | async-done | bytes 1280016 | tf_op jit(solution)/shard_map/all_gather | solution.py:413
  46.9 126.5 %shard_map.152 = (bf16[8,128,1600]{2,1,0:T(8,128)(2,1)}, bf16[8,128,1600]{2,1,0:T(8,128)(2,1)}, f32[4,8,8,256]{3,2,1,0:T(8,128)S(1)}, bf16[8,128,1600]{2,1,0:T(8...) custom-call(bf16[128,1600]{1,0:T(8,128)(2,1)S(1)} %bitcast.66, ...), custom_call_target="tpu_custom_call" | custom-call | tf_op jit(solution)/shard_map/pallas_call | solution.py:931
  174.6 10.8 %fusion.75 = (f32[1024]{0:T(1024)S(1)}, f32[1024,1600]{1,0:T(8,128)S(1)}) fusion(f32[1600]{0:T(1024)S(1)} %get-tuple-element.80, bf16[1600,1600]{1,0:T(8,128)(2,1)} %all-gather.8.cloned.1.call-done, bf16[1024,1792]{1,0:T(8,128)(2,1)} %get-tuple-element.20, bf16[1024,1600]{1,0:T(8,128)(2,1)} %bitcast.75), kind=kOutput, calls=%fused_computation.142 | convolution fusion | flops 5249432576 | bytes 18704640 | tf_op jit(solution)/shard_map/dot_general | solution.py:1050
  199.9 5.2 convolution_convert_fusion.1
  205.2 5.5 copy.75
  210.8 43.0 %reduce-scatter.9.cloned.1.call-done = bf16[128,1600]{1,0:T(8,128)(2,1)} async-done(((bf16[1024,1600]{1,0:T(8,128)(2,1)}), bf16[128,1600]{1,0:T(8,128)(2,1)}) %reduce-scatter.9.cloned.1.call-update) | async-done | bytes 409616 | tf_op jit(solution)/shard_map/reduce_scatter | solution.py:421
  259.8 38.1 %all-gather.10.cloned.1.call-done = bf16[1024,1600]{1,0:T(8,128)(2,1)} async-done(((bf16[128,1600]{1,0:T(8,128)(2,1)}), bf16[1024,1600]{1,0:T(8,128)(2,1)}) %all-gather.10.cloned.1.call-update) | async-done | bytes 3276816 | tf_op jit(solution)/shard_map/all_gather | solution.py:413
  301.5 11.7 %shard_map.153 = f32[1024,768]{1,0:T(8,128)} custom-call(bf16[1024,768]{1,0:T(8,128)(2,1)S(1)} %copy-done.5, bf16[1024,256]{1,0:T(8,128)(2,1)S(1)} %copy-done.7, bf16[1024,256]{1,0:T(8,128)(2,1)S(1)} %convolution_convert_fusion.6.refs_2_, f32[4,1024,1]{2,1,0:T(8,128)S(1)} %copy-done.3, f32[1024,1]{1,0:T(8,128)S(1)} %copy-done.4, ...), custom_call_target="tpu_custom_call" | custom-call | tf_op jit(solution)/shard_map/pallas_call | solution.py:395
  313.2 6.2 convolution_convert_fusion.5
  319.7 8.7 %convolution_convert_fusion.3 = bf16[832,1600]{1,0:T(8,128)(2,1)} fusion(bf16[1024,1600]{1,0:T(8,128)(2,1)} %bitcast.72, f32[1024,832]{0,1:T(8,128)} %copy-done.25, f32[832]{0:T(1024)S(1)} %add.268), kind=kOutput, calls=%fused_computation.11 | convolution fusion | flops 2736148480 | bytes 9350400 | tf_op jit(solution)/shard_map/dot_general | solution.py:329
  328.4 7.7 %convolution_convert_fusion.4 = bf16[832,1600]{1,0:T(8,128)(2,1)} fusion(f32[1024,1600]{1,0:T(8,128)} %copy-done.9, f32[1600]{0:T(1024)S(1)} %get-tuple-element.78, f32[1600]{0:T(1024)S(1)} %get-tuple-element.79, bf16[1024,832]{0,1:T(8,128)(2,1)S(1)} %copy-done.27), kind=kOutput, calls=%fused_computation.12 | convolution fusion | flops 2732544000 | bytes 10932736 | tf_op jit(solution)/shard_map/dot_general | solution.py:329
  336.2 8.9 %convolution_convert_fusion.2 = bf16[1024,1600]{0,1:T(8,128)(2,1)} fusion(bf16[832,1600]{1,0:T(8,128)(2,1)} %bitcast.76, f32[1024,832]{0,1:T(8,128)} %copy-done.25, f32[832]{0:T(1024)S(1)} %add.268), kind=kOutput, calls=%fused_computation.10 | convolution fusion | flops 2736455680 | bytes 9350400 | tf_op jit(solution)/shard_map/dot_general | solution.py:1065
  345.1 5.5 copy.74
  355.4 7.2 convolution_convert_fusion
  362.5 5.5 copy.77
  372.4 114.1 %all-reduce.16.cloned.1.call-done = (bf16[832,1600]{1,0:T(8,128)(2,1)}, bf16[832,1600]{1,0:T(8,128)(2,1)}) async-done(((bf16[832,1600]{1,0:T(8,128)(2,1)}, bf16[832,1600]{1,0:T(8,128)(2,1)}), (bf16[832,1600]{1,0:T(8,128)(2,1)}, bf16[832,1600]{1,0:T(8,128)(2,1)})) %all-reduce.16.cloned.1.call-update) | async-done | bytes 5324816
  489.6 42.3 %reduce-scatter.7.cloned.1.call-done = bf16[128,1600]{1,0:T(8,128)(2,1)} async-done(((bf16[1024,1600]{1,0:T(8,128)(2,1)}), bf16[128,1600]{1,0:T(8,128)(2,1)}) %reduce-scatter.7.cloned.1.call-update) | async-done | bytes 409616 | tf_op jit(solution)/shard_map/reduce_scatter | solution.py:421
  536.9 23.4 %reduce-scatter.15.cloned.1.call-done = bf16[400,200]{1,0:T(8,128)(2,1)} async-done(((bf16[1600,200]{1,0:T(8,128)(2,1)}), bf16[400,200]{1,0:T(8,128)(2,1)}) %reduce-scatter.15.cloned.1.call-update) | async-done | bytes 160016 | tf_op jit(solution)/shard_map/reduce_scatter | solution.py:427
  562.0 43.2 %reduce-scatter.11.cloned.1.call-done = bf16[128,1600]{1,0:T(8,128)(2,1)} async-done(((bf16[1024,1600]{1,0:T(8,128)(2,1)}), bf16[128,1600]{1,0:T(8,128)(2,1)}) %reduce-scatter.11.cloned.1.call-update) | async-done | bytes 409616 | tf_op jit(solution)/shard_map/reduce_scatter | solution.py:421
  610.5 28.0 %all-reduce.9 = bf16[8,1600]{1,0:T(8,128)(2,1)S(1)} all-reduce(bf16[8,1600]{1,0:T(8,128)(2,1)S(1)} %stack.44), channel_id=10, replica_groups=mesh['fsdp'=4,'seq'=8] {'seq'}, use_global_device_ids=true, to_apply=%region_22.23.clone | all-reduce | flops 12800 | bytes 51200
  638.6 9.9 %all-reduce.12 = (bf16[8,200]{1,0:T(8,128)(2,1)S(1)}, bf16[832]{0:T(1024)(128)(2,1)S(1)}) all-reduce(bf16[8,200]{1,0:T(8,128)(2,1)S(1)} %constant_dynamic-slice_fusion.1, bf16[832]{0:T(1024)(128)(2,1)S(1)} %get-tuple-element.97), channel_id=11, replica_groups=mesh['fsdp'=4,'seq'=8] {'fsdp'}, use_global_device_ids=true, to_apply=%region_23.24.clone | all-reduce | flops 2432 | bytes 9728
  649.7 9.4 %all-gather.12.cloned.1.call-done = bf16[3200,768]{1,0:T(8,128)(2,1)} async-done(((bf16[400,768]{1,0:T(8,128)(2,1)}), bf16[3200,768]{1,0:T(8,128)(2,1)}) %all-gather.12.cloned.1.call-update) | async-done | bytes 4915216 | tf_op jit(solution)/shard_map/all_gather | solution.py:1094
  680.7 13.9 %reshape.176 = bf16[8,400,3,256]{3,2,1,0:T(4,128)(2,1)} reshape(bf16[3200,768]{1,0:T(8,128)(2,1)} %all-gather.12.cloned.1.call-done) | data formatting | bytes 9830400 | tf_op jit(solution)/shard_map/reshape | solution.py:1094
  696.6 11.1 %reshape.160 = bf16[400,4800]{1,0:T(8,128)(2,1)} reshape(bf16[400,3,1600]{2,1,0:T(4,128)(2,1)} %fusion.43) | data formatting | bytes 7680000 | tf_op jit(solution)/shard_map/reshape | solution.py:1097
  (170 shorter events, 85.0 us)
Async XLA Ops:
  7.2 37.6 %copy-start = (bf16[400,600]{1,0:T(8,128)(2,1)S(1)}, bf16[400,600]{1,0:T(8,128)(2,1)}, u32[]{:S(2)}) copy-start(bf16[400,600]{1,0:T(8,128)(2,1)} %param.12) | copy-start | bytes 1440004
  7.2 34.9 %copy-start.21 = (s32[1,128]{1,0:T(1,128)S(1)}, s32[1,128]{1,0:T(1,128)}, u32[]{:S(2)}) copy-start(s32[1,128]{1,0:T(1,128)} %param.10) | copy-start | bytes 1540
  7.2 34.9 %copy-start.22 = (bf16[200]{0:T(256)(128)(2,1)S(1)}, bf16[200]{0:T(256)(128)(2,1)}, u32[]{:S(2)}) copy-start(bf16[200]{0:T(256)(128)(2,1)} %param.17) | copy-start | bytes 1204
  7.2 34.9 %copy-start.15 = (bf16[1,128,1600]{1,2,0:T(8,128)(2,1)S(1)}, bf16[1,128,1600]{1,2,0:T(8,128)(2,1)}, u32[]{:S(2)}) copy-start(bf16[1,128,1600]{1,2,0:T(8,128)(2,1)} %param.9) | copy-start | bytes 1228804
  7.2 35.2 %copy-start.13 = (bf16[1,128,1600]{1,2,0:T(8,128)(2,1)S(1)}, bf16[1,128,1600]{1,2,0:T(8,128)(2,1)}, u32[]{:S(2)}) copy-start(bf16[1,128,1600]{1,2,0:T(8,128)(2,1)} %param.11) | copy-start | bytes 1228804
  7.2 35.4 %copy-start.14 = (bf16[1600,200]{0,1:T(8,128)(2,1)S(1)}, bf16[1600,200]{0,1:T(8,128)(2,1)}, u32[]{:S(2)}) copy-start(bf16[1600,200]{0,1:T(8,128)(2,1)} %param.14) | copy-start | bytes 1920004
  7.2 31.2 %all-gather.6.cloned.1.call-start = ((), (), s32[]{:S(2)}) async-start(), calls=%async_computation.5 | async-start | bytes 1843200 | tf_op jit(solution)/shard_map/all_gather | solution.py:413
  9.2 165.4 %all-gather.8.cloned.1.call-start = ((), (), s32[]{:S(2)}) async-start(), calls=%async_computation.6 | async-start | bytes 6656000 | tf_op jit(solution)/shard_map/all_gather | solution.py:417
  41.9 211.8 %reduce-scatter.9.cloned.1.call-start = ((), (), s32[]{:S(2)}) async-start(), calls=%async_computation.8 | async-start | bytes 3833856 | tf_op jit(solution)/shard_map/reduce_scatter | solution.py:421
  188.8 4.8 copy-start.9
  193.6 5.0 copy-start.25
  210.7 87.3 %all-gather.10.cloned.1.call-start = ((), (), s32[]{:S(2)}) async-start(), calls=%async_computation.9 | async-start | bytes 3833856 | tf_op jit(solution)/shard_map/all_gather | solution.py:413
  258.7 109.5 %reduce-scatter.13.cloned.1.call-start = ((), (), s32[]{:S(2)}) async-start(), calls=%async_computation.11 | async-start | bytes 3072000 | tf_op jit(solution)/shard_map/reduce_scatter | solution.py:427
  259.8 41.6 %copy-start.3 = (f32[4,1024,1]{2,1,0:T(8,128)S(1)}, f32[4,1024,1]{2,1,0:T(8,128)}, u32[]{:S(2)}) copy-start(f32[4,1024,1]{2,1,0:T(8,128)} %get-tuple-element.27.refs_3_) | copy-start | bytes 49156
  301.5 11.7 %copy-start.18 = (bf16[8,128,1600]{2,1,0:T(8,128)(2,1)S(1)}, bf16[8,128,1600]{2,1,0:T(8,128)(2,1)}, u32[]{:S(2)}) copy-start(bf16[8,128,1600]{2,1,0:T(8,128)(2,1)} %get-tuple-element.29) | copy-start | bytes 9830404
  319.4 9.0 %copy-start.27 = (bf16[1024,832]{0,1:T(8,128)(2,1)S(1)}, bf16[1024,832]{0,1:T(8,128)(2,1)}, u32[]{:S(2)}) copy-start(bf16[1024,832]{0,1:T(8,128)(2,1)} %copy-done.26) | copy-start | bytes 5111812
  319.4 167.1 %all-reduce.16.cloned.1.call-start = ((), (), s32[]{:S(2)}) async-start(), calls=%async_computation.14 | async-start | bytes 11075584
  336.1 195.7 %reduce-scatter.7.cloned.1.call-start = ((), (), s32[]{:S(2)}) async-start(), calls=%async_computation.7 | async-start | bytes 3833856 | tf_op jit(solution)/shard_map/reduce_scatter | solution.py:421
  350.6 209.7 %reduce-scatter.15.cloned.1.call-start = ((), (), s32[]{:S(2)}) async-start(), calls=%async_computation.12 | async-start | bytes 1024000 | tf_op jit(solution)/shard_map/reduce_scatter | solution.py:427
  355.1 250.2 %reduce-scatter.11.cloned.1.call-start = ((), (), s32[]{:S(2)}) async-start(), calls=%async_computation.10 | async-start | bytes 3833856 | tf_op jit(solution)/shard_map/reduce_scatter | solution.py:421
  368.1 291.0 %all-gather.12.cloned.1.call-start = ((), (), s32[]{:S(2)}) async-start(), calls=%async_computation.13 | async-start | bytes 5529600 | tf_op jit(solution)/shard_map/all_gather | solution.py:1094
  486.5 47.9 %copy-start.12 = (bf16[128,1600]{1,0:T(8,128)(2,1)S(1)}, bf16[128,1600]{1,0:T(8,128)(2,1)}, u32[]{:S(2)}) copy-start(bf16[128,1600]{1,0:T(8,128)(2,1)} %reduce-scatter.9.cloned.1.call-done) | copy-start | bytes 1228804
  533.2 74.6 %copy-start.11 = (f32[128,1600]{1,0:T(8,128)S(1)}, f32[128,1600]{1,0:T(8,128)}, u32[]{:S(2)}) copy-start(f32[128,1600]{1,0:T(8,128)} %copy-done.10) | copy-start | bytes 2457604
  694.6 15.3 %copy-start.1 = (bf16[400,600]{1,0:T(8,128)(2,1)S(1)}, bf16[400,600]{1,0:T(8,128)(2,1)}, u32[]{:S(2)}) copy-start(bf16[400,600]{1,0:T(8,128)(2,1)} %param.12) | copy-start | bytes 1440004
  (14 other events, 32.0 us)
Sparse Core Ops, SparseCore 0:
  10.3 28.1 all-gather.5
  42.1 97.3 all-gather.7
  210.8 42.9 reduce-scatter.8
  258.8 39.0 all-gather.9
  319.5 37.0 reduce-scatter.12
  360.1 126.4 all-reduce.15
  488.8 42.9 reduce-scatter.6
  535.3 24.9 reduce-scatter.14
  562.6 42.5 reduce-scatter.10
  606.7 52.2 all-gather.11

commit v2 on v1

--- a/solution.py
+++ b/solution.py
@@ -344,89 +344,12 @@
         yield start, first, start + tile - first
 
 
-def allowed_pairs(ids_col, ids_row, start, first, tile, count):
-    q_pos = start + lax.broadcasted_iota(jnp.int32, (tile, count), 0)
-    k_pos = first + lax.broadcasted_iota(jnp.int32, (tile, count), 1)
-    return (k_pos <= q_pos) & (ids_col[start : start + tile, :1] == ids_row[:1, first : first + count])
-
-
-def attention_backward_kernel(
-    tile, reach, qkv_ref, attn_ref, grad_ref, lse_ref, ids_col, ids_row, out_ref
-):
-    head = pl.program_id(0)
-    length, span = attn_ref.shape
-    scale = HEAD_DIM**-0.5
-
-    @pl.when(head == 0)
-    def _():
-        out_ref[...] = jnp.zeros_like(out_ref)
-
-    for start, first, count in tile_pairs(length, tile, reach):
-        rows, keys = pl.ds(start, tile), pl.ds(first, count)
-        query = only_head(qkv_ref[rows, :span], head)
-        key = qkv_ref[keys, span : 2 * span]
-        grad = only_head(grad_ref[rows, :], head)
-        delta = jnp.sum(
-            grad.astype(jnp.float32) * attn_ref[rows, :].astype(jnp.float32), axis=1, keepdims=True
-        )
-        scores = contract_last(query, key) * scale
-        allowed = allowed_pairs(ids_col, ids_row, start, first, tile, count)
-        probs = jnp.where(allowed, jnp.exp(scores - lse_ref[0, rows, :]), 0.0)
-        prob_grad = contract_last(grad, qkv_ref[keys, 2 * span :])
-        score_grad = (probs * (prob_grad - delta)).astype(jnp.bfloat16)
-        out_ref[rows, :span] += scale * jnp.dot(
-            score_grad, only_head(key, head), preferred_element_type=jnp.float32
-        )
-        out_ref[keys, span : 2 * span] += scale * contract_first(score_grad, query)
-        out_ref[keys, 2 * span :] += contract_first(probs.astype(jnp.bfloat16), grad)
-
-
-def whole(shape):
-    return pl.BlockSpec(shape, lambda head: (0,) * len(shape))
-
-
-def per_head(shape):
-    return pl.BlockSpec((1,) + shape, lambda head: (head,) + (0,) * len(shape))
-
-
-def attention_backward(qkv, attn, grad, lse, ids_col, ids_row, reach):
-    length, span = attn.shape
-    tile = min(256, length)
-    return pl.pallas_call(
-        lambda *refs: attention_backward_kernel(tile, reach, *refs),
-        grid=(lse.shape[0],),
-        in_specs=[
-            whole(qkv.shape),
-            whole(attn.shape),
-            whole(grad.shape),
-            per_head((length, 1)),
-            whole(ids_col.shape),
-            whole(ids_row.shape),
-        ],
-        out_specs=whole(qkv.shape),
-        out_shape=jax.ShapeDtypeStruct(qkv.shape, jnp.float32),
-        compiler_params=pltpu.CompilerParams(vmem_limit_bytes=48 * 1024 * 1024),
-    )(qkv, attn, grad, lse, ids_col, ids_row)
-
-
 def join_seq(block, axis=0):
     return lax.all_gather(block, "seq", axis=axis, tiled=True)
 
 
 def join_fsdp(block, axis=0):
     return lax.all_gather(block, "fsdp", axis=axis, tiled=True)
-
-
-def sum_seq(terms, axis=0):
-    return lax.psum_scatter(
-        terms.astype(jnp.bfloat16), "seq", scatter_dimension=axis, tiled=True
-    ).astype(jnp.float32)
-
-
-def sum_fsdp(terms, axis=0):
-    return lax.psum_scatter(
-        terms.astype(jnp.bfloat16), "fsdp", scatter_dimension=axis, tiled=True
-    ).astype(jnp.float32)
 
 
 MESH = pl.DeviceIdType.MESH
@@ -619,7 +542,8 @@
     value = only_head(qkv_ref[keys, 2 * span :], head)
     mixed = jnp.dot(probs, value, preferred_element_type=jnp.float32)
     out_ref[rows, :] += mixed.astype(jnp.bfloat16)
-    lse_ref[head, rows, :] = top + jnp.log(total)
+    lane = lax.broadcasted_iota(jnp.int32, (tile, lse_ref.shape[1]), 1)
+    lse_ref[rows, :] = jnp.where(lane == head, top + jnp.log(total), lse_ref[rows, :])
 
 
 def attention_kernel(
@@ -633,6 +557,9 @@
     x_all,
     cot_all,
     small_all,
+    vec_all,
+    col_all,
+    row_all,
     h1_all,
     qkv_all,
     w_all,
@@ -722,8 +649,11 @@
         def _():
             remote(blocks_ref.at[k], place, piece_sent.at[k], landed, "seq", target).start()
 
-    x_line = RowGather(lambda c: x_ref, lambda i, c: x_v.at[i], x_sent, x_landed, row)
-    own_x = pltpu.make_async_copy(x_ref, x_v.at[seq], local_sem.at[0])
+    def block_of(target):
+        return lambda i, c: target.at[pl.ds(pl.multiple_of(i * own_rows, own_rows), own_rows)]
+
+    x_line = RowGather(lambda c: x_ref, block_of(x_v), x_sent, x_landed, row)
+    own_x = pltpu.make_async_copy(x_ref, block_of(x_v)(seq, 0), local_sem.at[0])
     own_x.start()
     used.append(None)
     x_line.start()
@@ -809,9 +739,9 @@
     proj_plane.start()
     x_line.pass_on(2)
     x_line.pass_on(3)
-    cot_line = RowGather(lambda c: cot_ref, lambda i, c: cot_all.at[i], cot_sent, cot_landed, row)
+    cot_line = RowGather(lambda c: cot_ref, block_of(cot_all), cot_sent, cot_landed, row)
     cot_line.start()
-    keep(cot_ref, cot_all.at[seq])
+    keep(cot_ref, block_of(cot_all)(seq, 0))
     keep(fc_ref, fc_all.at[fsdp])
     keep(proj_ref, proj_all.at[fsdp])
     x_line.from_other_core()
@@ -821,10 +751,10 @@
     query_shift, value_shift = vec[2:3, lanes], vec[3:4, lanes]
 
     def project(i, carry):
-        hidden = norm_rows(x_v[i].astype(jnp.float32), vec[0:1, :width], vec[1:2, :width])
+        rows = pl.ds(pl.multiple_of(i * own_rows, own_rows), own_rows)
+        hidden = norm_rows(x_v[rows, :].astype(jnp.float32), vec[0:1, :width], vec[1:2, :width])
         hidden = hidden.astype(jnp.bfloat16)
-        h1_v[i] = hidden
-        rows = pl.ds(pl.multiple_of(i * own_rows, own_rows), own_rows)
+        h1_v[rows, :] = hidden
         mixed = jnp.dot(hidden, w_v[...], preferred_element_type=jnp.float32)
         qkv_v[rows, :span] = (mixed[:, :span] + query_shift).astype(jnp.bfloat16)
         qkv_v[rows, span : 2 * span] = mixed[:, span : 2 * span].astype(jnp.bfloat16)
@@ -835,11 +765,15 @@
     cot_line.pass_on(1)
     keep(x_v, x_all)
     keep(small_v, small_all)
+    keep(vec, vec_all)
+    keep(ids_col, col_all)
+    keep(ids_row, row_all)
     keep(h1_v, h1_all)
     keep(qkv_v, qkv_all)
     keep(w_v, w_all)
 
     attn_v[...] = jnp.zeros_like(attn_v)
+    lse_all[...] = jnp.zeros_like(lse_all)
     tile = 256
 
     def heads(h, carry):
@@ -931,29 +865,32 @@
     return pl.pallas_call(
         lambda *refs: attention_kernel(reach, *refs),
         out_shape=[
-            shaped(row, own_rows, width),
-            shaped(row, own_rows, width),
+            shaped(length, width),
+            shaped(length, width),
             shaped(plane, row, 8, span, dtype=f32),
-            shaped(row, own_rows, width),
+            shaped(8, 8 * span, dtype=f32),
+            shaped(length, own_rows, dtype=f32),
+            shaped(8, length, dtype=f32),
+            shaped(length, width),
             shaped(length, 3 * span),
             shaped(width, 3 * span),
-            shaped(4, length, 1, dtype=f32),
+            shaped(length, 128, dtype=f32),
             shaped(length, span),
             shaped(length, 7 * span),
             shaped(plane, units, width),
             shaped(plane, units, width),
         ],
         in_specs=[anywhere] * 6,
-        out_specs=[anywhere] * 6 + [in_vmem] + [anywhere] * 4,
+        out_specs=[anywhere] * 9 + [in_vmem] + [anywhere] * 4,
         scratch_shapes=[
-            pltpu.VMEM((row, own_rows, width), bf),
+            pltpu.VMEM((length, width), bf),
             pltpu.VMEM((plane, row, 8, span), f32),
             pltpu.VMEM((8, 8 * span), f32),
             pltpu.VMEM((length, own_rows), f32),
             pltpu.VMEM((8, length), f32),
             pltpu.VMEM((3, 2, width // plane, span), bf),
             pltpu.VMEM((width, 3 * span), bf),
-            pltpu.VMEM((row, own_rows, width), bf),
+            pltpu.VMEM((length, width), bf),
             pltpu.VMEM((length, 3 * span), bf),
             pltpu.VMEM((length, span), bf),
             dma((row - 1,)),
@@ -974,7 +911,7 @@
             dma((4,)),
             dma((4,)),
             dma((4,)),
-            dma((12,)),
+            dma((16,)),
         ],
         compiler_params=pltpu.CompilerParams(
             collective_id=0, has_side_effects=True, vmem_limit_bytes=50 * 1024 * 1024
@@ -982,15 +919,794 @@
     )(x_own, cot_own, small, blocks, fc_own, proj_own)
 
 
-def column_blocks(shard, own, width, span):
-    columns = shard.shape[1]
+def pick(index, values):
+    chosen = values[-1]
+    for k in range(len(values) - 1):
+        chosen = jnp.where(index == k, values[k], chosen)
+    return chosen
+
+
+def chip_order(chip, step):
+    rows = ((3, 3, 0, 0), (2, 0, 3, 1), (1, 2, 1, 2), (0, 1, 2, 3))
+    return pick(step, [pick(chip, row) for row in rows])
+
+
+class RowSum:
+    def __init__(self, own, away, pair, chain, pair_sent, pair_landed, chain_sent, chain_landed):
+        self.own, self.away, self.pair, self.chain = own, away, pair, chain
+        self.pair_sent, self.pair_landed = pair_sent, pair_landed
+        self.chain_sent, self.chain_landed = chain_sent, chain_landed
+        self.me = lax.axis_index("seq")
+        self.chips = 4
+        self.chip, self.core = self.me // 2, self.me % 2
+        self.other = self.me + 1 - 2 * self.core
+
+    def exchange(self, t):
+        return remote(
+            self.away.at[t],
+            self.pair.at[t],
+            self.pair_sent.at[t],
+            self.pair_landed.at[t],
+            "seq",
+            self.other,
+        )
+
+    def onward(self, t, slot, target):
+        return remote(
+            self.own.at[t],
+            self.chain.at[slot],
+            self.chain_sent.at[t],
+            self.chain_landed.at[slot],
+            "seq",
+            target,
+        )
+
+    def put(self, t, terms):
+        rows = self.own.shape[1]
+        self.away[t] = terms[pl.ds(pl.multiple_of((1 - self.core) * rows, rows), rows), :].astype(
+            jnp.bfloat16
+        )
+        self.exchange(t).start()
+        self.own[t] = terms[pl.ds(pl.multiple_of(self.core * rows, rows), rows), :].astype(jnp.bfloat16)
+
+    def add(self, t, arrived, slot):
+        total = self.own[t].astype(jnp.float32) + arrived[slot].astype(jnp.float32)
+        self.own[t] = total.astype(jnp.bfloat16)
+
+    def step(self, t):
+        self.exchange(t).wait_recv()
+        self.add(t, self.pair, t)
+
+        def forward():
+            @pl.when(self.chip > 0)
+            def _():
+                self.onward(t, t, self.me + 2).wait_recv()
+                self.add(t, self.chain, t)
+
+            self.onward(t, t, self.me + 2).start()
+
+        def backward():
+            @pl.when(self.chip < self.chips - 1)
+            def _():
+                self.onward(t, t, self.me - 2).wait_recv()
+                self.add(t, self.chain, t)
+
+            slot = jnp.where(t == self.chip - 1, self.chips, t)
+            self.onward(t, slot, self.me - 2).start()
+
+        pl.when(t > self.chip)(forward)
+        pl.when(t < self.chip)(backward)
+
+    def final(self, total):
+        t = self.chip
+        self.exchange(t).wait_recv()
+        total[...] = self.own[t].astype(jnp.float32) + self.pair[t].astype(jnp.float32)
+
+        @pl.when(self.chip > 0)
+        def _():
+            self.onward(t, t, self.other).wait_recv()
+            total[...] += self.chain[t].astype(jnp.float32)
+
+        @pl.when(self.chip < self.chips - 1)
+        def _():
+            self.onward(t, self.chips, self.other).wait_recv()
+            total[...] += self.chain[self.chips].astype(jnp.float32)
+
+    def drain(self):
+        for t in range(self.chips):
+            self.exchange(t).wait_send()
+
+            @pl.when(self.chip != t)
+            def _():
+                self.onward(t, t, self.other).wait_send()
+
+
+class PlaneTerms:
+    def __init__(self, view, terms, sent, landed):
+        self.view, self.terms, self.sent, self.landed = view, terms, sent, landed
+        self.me = lax.axis_index("fsdp")
+
+    def to(self, ahead):
+        i = lax.rem(self.me + ahead, 4)
+        return remote(
+            self.view(i), self.terms.at[self.me], self.sent.at[ahead], self.landed.at[self.me], "fsdp", i
+        )
+
+    def keep(self):
+        return pltpu.make_async_copy(
+            self.view(self.me), self.terms.at[self.me], self.landed.at[self.me]
+        )
+
+    def start(self):
+        self.keep().start()
+        for ahead in (3, 1, 2):
+            self.to(ahead).start()
+
+    def arrive(self):
+        self.keep().wait()
+        for ahead in range(1, 4):
+            i = lax.rem(self.me + ahead, 4)
+            remote(
+                self.view(i), self.terms.at[i], self.sent.at[ahead], self.landed.at[i], "fsdp", i
+            ).wait_recv()
+
+    def drain(self):
+        for ahead in range(1, 4):
+            self.to(ahead).wait_send()
+
+
+def backward_attend(
+    head, start, first, count, tile, qkv_ref, attn_ref, grad_ref, lse_ref, ids_col, ids_row, out_ref
+):
+    span = attn_ref.shape[1]
+    scale = HEAD_DIM**-0.5
+    rows, keys = pl.ds(start, tile), pl.ds(first, count)
+    query = only_head(qkv_ref[rows, :span], head)
+    key = qkv_ref[keys, span : 2 * span]
+    grad = only_head(grad_ref[rows, :], head)
+    delta = jnp.sum(
+        grad.astype(jnp.float32) * attn_ref[rows, :].astype(jnp.float32), axis=1, keepdims=True
+    )
+    scores = contract_last(query, key) * scale
+    q_pos = start + lax.broadcasted_iota(jnp.int32, (tile, count), 0)
+    k_pos = first + lax.broadcasted_iota(jnp.int32, (tile, count), 1)
+    allowed = (k_pos <= q_pos) & (ids_col[rows, :1] == ids_row[:1, keys])
+    lane = lax.broadcasted_iota(jnp.int32, (tile, lse_ref.shape[1]), 1)
+    lse = jnp.sum(jnp.where(lane == head, lse_ref[rows, :], 0.0), axis=1, keepdims=True)
+    probs = jnp.where(allowed, jnp.exp(scores - lse), 0.0)
+    prob_grad = contract_last(grad, qkv_ref[keys, 2 * span :])
+    score_grad = (probs * (prob_grad - delta)).astype(jnp.bfloat16)
+    out_ref[rows, :span] += scale * jnp.dot(
+        score_grad, only_head(key, head), preferred_element_type=jnp.float32
+    )
+    out_ref[keys, span : 2 * span] += scale * contract_first(score_grad, query)
+    out_ref[keys, 2 * span :] += contract_first(probs.astype(jnp.bfloat16), grad)
+
+
+def row_tiles(count, size, body):
+    def step(i, carry):
+        body(pl.multiple_of(i * size, size))
+        return carry
+
+    lax.fori_loop(0, count // size, step, 0)
+
+
+def backward_kernel(
+    reach,
+    x_ref,
+    cot_ref,
+    vec_ref,
+    bias_ref,
+    w_attn_ref,
+    attn_ref,
+    fc_ref,
+    proj_ref,
+    h1_ref,
+    qkv_ref,
+    w_qkv_ref,
+    lse_ref,
+    attn_own_ref,
+    ids_col_ref,
+    ids_row_ref,
+    result_ref,
+    input_grad_ref,
+    fc_terms,
+    proj_terms,
+    attn_terms,
+    nat_blocks,
+    vec_out,
+    qkv_terms,
+    attn_v,
+    own1,
+    away1,
+    pair1,
+    chain1,
+    own2,
+    away2,
+    pair2,
+    chain2,
+    dr_all,
+    resid_own,
+    dresid_own,
+    total,
+    wide,
+    fc_stage,
+    proj_stage,
+    vec_v,
+    bias_v,
+    bias_sum,
+    gv,
+    vec_send,
+    vec_land,
+    plane_send,
+    plane_land,
+    pair_sent,
+    pair_landed,
+    chain_sent,
+    chain_landed,
+    dr_sent,
+    dr_landed,
+    terms_sent,
+    terms_landed,
+    nat_sent,
+    nat_landed,
+    vec_sent,
+    vec_landed,
+    plane_sent,
+    plane_landed,
+    load_sem,
+):
+    row, plane, chips = 8, 4, 4
+    seq, fsdp = lax.axis_index("seq"), lax.axis_index("fsdp")
+    chip, core = seq // 2, seq % 2
+    ends = (chip == 0) | (chip == chips - 1)
+    length, width = x_ref.shape
+    own_rows = length // row
+    pair_rows = 2 * own_rows
+    units = fc_ref.shape[1]
+    span = attn_own_ref.shape[1]
+    depth = width // plane
+    groups = -(-width // span)
+    group = group_of(seq)
+    columns = qkv_columns(width, row)
+    bf, f32 = jnp.bfloat16, jnp.float32
+    tiles = [(0, 512), (512, 1024), (1024, width)]
+
+    def load(source, target, slot):
+        copy = pltpu.make_async_copy(source, target, load_sem.at[slot])
+        copy.start()
+        return copy
+
+    def pair_at(t):
+        return pl.ds(pl.multiple_of(t * pair_rows, pair_rows), pair_rows)
+
+    own_at = pl.ds(pl.multiple_of(seq * own_rows, own_rows), own_rows)
+    half_at = pl.ds(pl.multiple_of(core * own_rows, own_rows), own_rows)
+    hidden_sum = RowSum(
+        own1, away1, pair1, chain1, pair_sent.at[0], pair_landed.at[0], chain_sent.at[0], chain_landed.at[0]
+    )
+    out_sum = RowSum(
+        own2, away2, pair2, chain2, pair_sent.at[1], pair_landed.at[1], chain_sent.at[1], chain_landed.at[1]
+    )
+    dr_line = RowGather(
+        None,
+        lambda i, c: dr_all.at[pl.ds(pl.multiple_of(i * own_rows, own_rows), own_rows)],
+        dr_sent,
+        dr_landed,
+        row,
+    )
+    fc_plane = PlaneTerms(lambda i: fc_stage.at[i], fc_terms, terms_sent.at[0], terms_landed.at[0])
+    proj_plane = PlaneTerms(lambda i: proj_stage.at[i], proj_terms, terms_sent.at[1], terms_landed.at[1])
+
+    def feed_forward(w_attn, x_v, cot_v, fc_v, proj_v, h2_v, act_v, dpre_v, pre_v, dact_v):
+        first = chip_order(chip, 0)
+        loads = [
+            load(attn_ref, attn_v, 0),
+            load(w_attn_ref.at[pl.ds(0, width)], w_attn, 1),
+            load(x_ref.at[pair_at(first)], x_v, 2),
+            load(vec_ref, vec_v, 3),
+            load(fc_ref, fc_v, 4),
+            load(cot_ref, cot_v, 5),
+            load(proj_ref, proj_v, 6),
+            load(bias_ref, bias_v, 7),
+        ]
+        bias_sum[...] = jnp.zeros_like(bias_sum)
+        gv[...] = jnp.zeros_like(gv)
+        greet(row, plane)
+        for copy in loads:
+            copy.wait()
+
+        def chunk(p, carry):
+            t = chip_order(chip, p)
+            rows = pair_at(t)
+            for low, high in tiles:
+                wide[:, low:high] = jnp.dot(
+                    attn_v[rows, :width], w_attn[:, low:high], preferred_element_type=f32
+                )
+
+            @pl.when(p > 0)
+            def _():
+                pltpu.make_async_copy(x_ref.at[rows], x_v, load_sem.at[2]).wait()
+
+            def second_norm(i):
+                part = pl.ds(i, 16)
+                resid = wide[part, :] + x_v[part, :].astype(f32) + vec_v[4:5, :width]
+                wide[part, :] = resid
+                hidden = norm_rows(resid, vec_v[5:6, :width], vec_v[6:7, :width])
+                h2_v[pl.ds(pl.multiple_of(t * pair_rows + i, 16), 16), :] = hidden.astype(bf)
+
+            row_tiles(pair_rows, 16, second_norm)
+
+            @pl.when(p < chips - 1)
+            def _():
+                load(x_ref.at[pair_at(chip_order(chip, p + 1))], x_v, 2)
+
+            @pl.when(t == chip)
+            def _():
+                resid_own[...] = wide[half_at, :]
+
+            def unit_block(f, carry):
+                pre_v[...] = contract_last(h2_v[rows, :], fc_v[f])
+                dact_v[...] = contract_last(cot_v[rows, :], proj_v[f])
+                shift = bias_v[pl.ds(f, 1), :units]
+
+                def gelu(i):
+                    part = pl.ds(i, 32)
+                    gelu_value, gelu_slope = gelu_parts(pre_v[part, :] + shift)
+                    dpre = dact_v[part, :] * gelu_slope
+                    place = pl.ds(pl.multiple_of(t * pair_rows + i, 32), 32)
+                    act_v[f, place, :] = gelu_value.astype(bf)
+                    dpre_v[f, place, :] = dpre.astype(bf)
+                    bias_sum[pl.ds(f, 1), :units] += jnp.sum(dpre, axis=0, keepdims=True)
+
+                row_tiles(pair_rows, 32, gelu)
+                return carry
+
+            lax.fori_loop(0, plane, unit_block, 0)
+
+            def back_through(values, weights):
+                for low, high in tiles:
+                    terms = jnp.dot(
+                        values[0, rows, :], weights[0, :, low:high], preferred_element_type=f32
+                    )
+                    for f in range(1, plane):
+                        terms += jnp.dot(
+                            values[f, rows, :], weights[f, :, low:high], preferred_element_type=f32
+                        )
+                    wide[:, low:high] = terms
+
+            back_through(dpre_v, fc_v)
+            hidden_sum.put(t, wide)
+            back_through(act_v, proj_v)
+            out_sum.put(t, wide)
+
+            @pl.when(ends & (p < chips - 1))
+            def _():
+                hidden_sum.step(t)
+
+            @pl.when(jnp.logical_not(ends) & (p == 2))
+            def _():
+                hidden_sum.step(chip_order(chip, 0))
+
+            return carry
+
+        lax.fori_loop(0, chips, chunk, 0)
+
+        @pl.when(jnp.logical_not(ends))
+        def _():
+            hidden_sum.step(chip_order(chip, 1))
+            hidden_sum.step(chip_order(chip, 2))
+
+        hidden_sum.final(total)
+
+        def second_norm_back(i):
+            part = pl.ds(i, 16)
+            resid = resid_own[part, :]
+            centred = resid - jnp.mean(resid, axis=-1, keepdims=True)
+            inverse = lax.rsqrt(jnp.mean(centred * centred, axis=-1, keepdims=True) + norm_eps)
+            normed = centred * inverse
+            grad_hidden = total[part, :]
+            scaled = grad_hidden * vec_v[5:6, :width]
+            back = inverse * (
+                scaled
+                - jnp.mean(scaled, axis=-1, keepdims=True)
+                - normed * jnp.mean(scaled * normed, axis=-1, keepdims=True)
+            )
+            place = pl.ds(pl.multiple_of(seq * own_rows + i, 16), 16)
+            cot = cot_v[place, :].astype(f32)
+            grad_resid = cot + back
+            dresid_own[part, :] = grad_resid
+            dr_all[place, :] = grad_resid.astype(bf)
+            for at, values in ((4, grad_resid), (5, grad_hidden * normed), (6, grad_hidden), (7, cot)):
+                gv[at : at + 1, :width] += jnp.sum(values, axis=0, keepdims=True)
+
+        row_tiles(own_rows, 16, second_norm_back)
+        dr_line.start()
+
+        @pl.when(ends)
+        def _():
+            for p in range(chips - 1):
+                out_sum.step(chip_order(chip, p))
+
+        def weight_terms(values, others, stage):
+            def unit_block(f, carry):
+                for low, high in tiles:
+                    stage[f, :, low:high] = contract_first(values[f], others[:, low:high]).astype(bf)
+                return carry
+
+            lax.fori_loop(0, plane, unit_block, 0)
+
+        weight_terms(act_v, cot_v, proj_stage)
+        proj_plane.start()
+        dr_line.pass_on(1)
+        weight_terms(dpre_v, h2_v, fc_stage)
+        fc_plane.start()
+        dr_line.pass_on(2)
+
+    pl.run_scoped(
+        feed_forward,
+        pltpu.VMEM((width, width), bf),
+        pltpu.VMEM((pair_rows, width), bf),
+        pltpu.VMEM((length, width), bf),
+        pltpu.VMEM((plane, units, width), bf),
+        pltpu.VMEM((plane, units, width), bf),
+        pltpu.VMEM((length, width), bf),
+        pltpu.VMEM((plane, length, units), bf),
+        pltpu.VMEM((plane, length, units), bf),
+        pltpu.VMEM((pair_rows, units), f32),
+        pltpu.VMEM((pair_rows, units), f32),
+    )
+
+    def attention_back(w_rows, h1_v, qkv_v, w_qkv, lse_v, attn_own, col_v, row_v, da_v, dqkv, dqkv16, ga, gq, gqt, own_x):
+        loads = [
+            load(w_attn_ref.at[pl.ds(pl.multiple_of(group * span, span), span)], w_rows, 0),
+            load(qkv_ref, qkv_v, 1),
+            load(lse_ref, lse_v, 2),
+            load(attn_own_ref, attn_own, 3),
+            load(ids_col_ref, col_v, 4),
+            load(ids_row_ref, row_v, 5),
+            load(h1_ref, h1_v, 6),
+            load(w_qkv_ref, w_qkv, 7),
+            load(x_ref.at[own_at], own_x, 8),
+        ]
+        dqkv[...] = jnp.zeros_like(dqkv)
+        dr_line.pass_on(3)
+        dr_line.from_other_core()
+        for copy in loads:
+            copy.wait()
+
+        def into_heads(i):
+            rows = pl.ds(i, pair_rows)
+            da_v[rows, :] = contract_last(dr_all[rows, :], w_rows[...]).astype(bf)
+
+        row_tiles(length, pair_rows, into_heads)
+
+        @pl.when(jnp.logical_not(ends))
+        def _():
+            out_sum.step(chip_order(chip, 0))
+
+        def heads(h, carry):
+            for start, first, count in tile_pairs(length, 256, reach):
+                backward_attend(
+                    h, start, first, count, 256, qkv_v, attn_own, da_v, lse_v, col_v, row_v, dqkv
+                )
+            return carry
+
+        lax.fori_loop(0, 2, heads, 0)
+
+        @pl.when(jnp.logical_not(ends))
+        def _():
+            out_sum.step(chip_order(chip, 1))
+
+        lax.fori_loop(2, 4, heads, 0)
+
+        @pl.when(jnp.logical_not(ends))
+        def _():
+            out_sum.step(chip_order(chip, 2))
+
+        lanes = pl.ds(pl.multiple_of(group * span, span), span)
+        gv[2:3, lanes] = jnp.sum(dqkv[:, :span], axis=0, keepdims=True)
+        gv[3:4, lanes] = jnp.sum(dqkv[:, 2 * span :], axis=0, keepdims=True)
+        dqkv16[...] = dqkv[...].astype(bf)
+
+        for low in range(0, width, span):
+            high = min(low + span, width)
+            gq[low:high, :] = contract_first(h1_v[:, low:high], dqkv16[...]).astype(bf)
+        qkv_plane = PlaneTerms(
+            lambda i: gq.at[pl.ds(pl.multiple_of(i * depth, 16), depth)],
+            qkv_terms,
+            terms_sent.at[2],
+            terms_landed.at[2],
+        )
+        qkv_plane.start()
+
+        hidden_sum.drain()
+
+        def chunk(p, carry):
+            t = chip_order(chip, p)
+            for low, high in tiles:
+                wide[:, low:high] = contract_last(dqkv16[pair_at(t), :], w_qkv[low:high, :])
+            hidden_sum.put(t, wide)
+
+            @pl.when(ends & (p < chips - 1))
+            def _():
+                hidden_sum.step(t)
+
+            return carry
+
+        lax.fori_loop(0, chips, chunk, 0)
+
+        share = width // row
+        place = lax.broadcasted_iota(jnp.int32, (width, span), 0)
+        lane = lax.broadcasted_iota(jnp.int32, (width, span), 1)
+        chosen = ((place == seq * share + lane) & (lane < share)).astype(f32).astype(bf)
+
+        def own_columns(i):
+            rows = pl.ds(i, pair_rows)
+            da_v[rows, :] = jnp.dot(dr_all[rows, :], chosen, preferred_element_type=f32).astype(bf)
+
+        row_tiles(length, pair_rows, own_columns)
+        for low in range(0, width, span):
+            high = min(low + span, width)
+            ga[low:high, :] = contract_first(attn_v[:, low:high], da_v[...]).astype(bf)
+        attn_plane = PlaneTerms(
+            lambda i: ga.at[pl.ds(pl.multiple_of(i * depth, 16), depth)],
+            attn_terms,
+            terms_sent.at[3],
+            terms_landed.at[3],
+        )
+        attn_plane.start()
+
+        @pl.when(jnp.logical_not(ends))
+        def _():
+            for p in range(chips - 1):
+                hidden_sum.step(chip_order(chip, p))
+
+        qkv_plane.arrive()
+        load(qkv_terms, gqt, 0).wait()
+        qkv_plane.drain()
+        for kind in range(3):
+            part = gqt[0, :, kind * span : (kind + 1) * span].astype(f32)
+            for f in range(1, plane):
+                part += gqt[f, :, kind * span : (kind + 1) * span].astype(f32)
+            gq[kind * depth : (kind + 1) * depth, :span] = part.astype(bf)
+
+        def nat(kind, late):
+            begins = kind * width + group * span
+            last = begins + jnp.minimum(span, width - group * span) - 1
+            before, after = begins // columns, last // columns
+            target = after if late else before
+            slot = kind * groups + group - own_blocks(target, columns, width, span)[0]
+            there = (group < groups) & (before != after) if late else group < groups
+            return there, target, slot
+
+        def nat_copy(kind, late, target, slot):
+            return remote(
+                gq.at[pl.ds(kind * depth, depth), pl.ds(0, span)],
+                nat_blocks.at[slot],
+                nat_sent.at[kind, late],
+                nat_landed.at[slot],
+                "seq",
+                target,
+            )
+
+        for kind in range(3):
+            for late in range(2):
+                there, target, slot = nat(kind, late)
+
+                @pl.when(there & (target != seq))
+                def _():
+                    nat_copy(kind, late, target, slot).start()
+
+                @pl.when(there & (target == seq))
+                def _():
+                    pltpu.make_async_copy(
+                        gq.at[pl.ds(kind * depth, depth), pl.ds(0, span)],
+                        nat_blocks.at[slot],
+                        nat_landed.at[slot],
+                    ).start()
+
+        hidden_sum.final(total)
+
+        def first_norm_back(i):
+            part = pl.ds(i, 16)
+            values = own_x[part, :].astype(f32)
+            centred = values - jnp.mean(values, axis=-1, keepdims=True)
+            inverse = lax.rsqrt(jnp.mean(centred * centred, axis=-1, keepdims=True) + norm_eps)
+            normed = centred * inverse
+            grad_hidden = total[part, :]
+            scaled = grad_hidden * vec_v[0:1, :width]
+            back = inverse * (
+                scaled
+                - jnp.mean(scaled, axis=-1, keepdims=True)
+                - normed * jnp.mean(scaled * normed, axis=-1, keepdims=True)
+            )
+            input_grad_ref[part, :] = dresid_own[part, :] + back
+            for at, summed in ((0, grad_hidden * normed), (1, grad_hidden)):
+                gv[at : at + 1, :width] += jnp.sum(summed, axis=0, keepdims=True)
+
+        row_tiles(own_rows, 16, first_norm_back)
+
+        vec_send[...] = jnp.zeros_like(vec_send)
+        plane_send[...] = jnp.zeros_like(plane_send)
+        for i in range(row):
+            vec_send[i, :, :share] = gv[:, share * i : share * (i + 1)]
+
+        def vec_to(ahead):
+            i = lax.rem(seq + ahead, row)
+            return remote(
+                vec_send.at[i], vec_land.at[seq], vec_sent.at[ahead], vec_landed.at[seq], "seq", i
+            )
+
+        keep = pltpu.make_async_copy(vec_send.at[seq], vec_land.at[seq], vec_landed.at[seq])
+        keep.start()
+        for ahead in range(1, row):
+            vec_to(ahead).start()
+        out_sum.final(total)
+        for low, high in tiles:
+            result_ref[:, low:high] = (
+                resid_own[:, low:high] + total[:, low:high] + vec_v[7:8, low:high]
+            )
+        for i in range(row):
+            pltpu.make_async_copy(vec_send.at[i], vec_land.at[i], vec_landed.at[i]).wait()
+        summed = vec_land[0]
+        for i in range(1, row):
+            summed += vec_land[i]
+        for i in range(plane):
+            plane_send[i, 0:2, :] = summed[2 * i : 2 * i + 2, :]
+            plane_send[i, 2:3, :] = bias_sum[i : i + 1, :]
+        vec_plane = PlaneTerms(lambda i: plane_send.at[i], plane_land, plane_sent, plane_landed)
+        vec_plane.start()
+        first_block, last_block = own_blocks(seq, columns, width, span)
+        for k in range(4):
+
+            @pl.when(first_block + k <= last_block)
+            def _():
+                pltpu.make_async_copy(
+                    gq.at[pl.ds(0, depth), pl.ds(0, span)], nat_blocks.at[k], nat_landed.at[k]
+                ).wait()
+
+        vec_plane.arrive()
+        vec_out[...] = plane_land[0] + plane_land[1] + plane_land[2] + plane_land[3]
+        vec_plane.drain()
+        for ahead in range(1, row):
+            vec_to(ahead).wait_send()
+        for kind in range(3):
+            for late in range(2):
+                there, target, slot = nat(kind, late)
+
+                @pl.when(there & (target != seq))
+                def _():
+                    nat_copy(kind, late, target, slot).wait_send()
+
+        attn_plane.drain()
+        attn_plane.arrive()
+
+    pl.run_scoped(
+        attention_back,
+        pltpu.VMEM((span, width), bf),
+        pltpu.VMEM((length, width), bf),
+        pltpu.VMEM((length, 3 * span), bf),
+        pltpu.VMEM((width, 3 * span), bf),
+        pltpu.VMEM((length, 128), f32),
+        pltpu.VMEM((length, span), bf),
+        pltpu.VMEM((length, 128), f32),
+        pltpu.VMEM((8, length), f32),
+        pltpu.VMEM((length, span), bf),
+        pltpu.VMEM((length, 3 * span), f32),
+        pltpu.VMEM((length, 3 * span), bf),
+        pltpu.VMEM((width, span), bf),
+        pltpu.VMEM((width, 3 * span), bf),
+        pltpu.VMEM((plane, depth, 3 * span), bf),
+        pltpu.VMEM((own_rows, width), bf),
+    )
+    for summing in (hidden_sum, out_sum):
+        summing.drain()
+    dr_line.drain()
+    for terms in (fc_plane, proj_plane):
+        terms.drain()
+        terms.arrive()
+
+
+def backward_phase(
+    x_all, cot_all, vec, bias, w_attn, attn_all, w_fc, w_proj, h1_all, qkv, w_qkv, lse, attn_own, ids_col, ids_row, reach
+):
+    length, width = x_all.shape
+    row, plane, chips, span = 8, 4, 4, attn_own.shape[1]
+    own_rows, units, depth = length // row, w_fc.shape[1], width // plane
+    bf, f32 = jnp.bfloat16, jnp.float32
+    anywhere = pl.BlockSpec(memory_space=pl.ANY)
+    in_vmem = pl.BlockSpec(memory_space=pltpu.VMEM)
+    dma = pltpu.SemaphoreType.DMA
+
+    def shaped(*shape, dtype=bf):
+        return jax.ShapeDtypeStruct(shape, dtype)
+
+    block = (own_rows, width)
+    return pl.pallas_call(
+        lambda *refs: backward_kernel(reach, *refs),
+        out_shape=[
+            shaped(*block, dtype=f32),
+            shaped(*block, dtype=f32),
+            shaped(plane, units, width),
+            shaped(plane, units, width),
+            shaped(plane, depth, span),
+            shaped(4, depth, span),
+            shaped(8, span, dtype=f32),
+            shaped(plane, depth, 3 * span),
+        ],
+        in_specs=[anywhere] * 15,
+        out_specs=[in_vmem] * 2 + [anywhere] * 4 + [in_vmem] + [anywhere],
+        scratch_shapes=[
+            pltpu.VMEM(attn_all.shape, bf),
+            pltpu.VMEM((chips,) + block, bf),
+            pltpu.VMEM((chips,) + block, bf),
+            pltpu.VMEM((chips,) + block, bf),
+            pltpu.VMEM((chips + 1,) + block, bf),
+            pltpu.VMEM((chips,) + block, bf),
+            pltpu.VMEM((chips,) + block, bf),
+            pltpu.VMEM((chips,) + block, bf),
+            pltpu.VMEM((chips + 1,) + block, bf),
+            pltpu.VMEM((length, width), bf),
+            pltpu.VMEM(block, f32),
+            pltpu.VMEM(block, f32),
+            pltpu.VMEM(block, f32),
+            pltpu.VMEM((2 * own_rows, width), f32),
+            pltpu.VMEM((plane, units, width), bf),
+            pltpu.VMEM((plane, units, width), bf),
+            pltpu.VMEM((8, 8 * span), f32),
+            pltpu.VMEM((8, span), f32),
+            pltpu.VMEM((8, span), f32),
+            pltpu.VMEM((8, 8 * span), f32),
+            pltpu.VMEM((row, 8, span), f32),
+            pltpu.VMEM((row, 8, span), f32),
+            pltpu.VMEM((plane, 8, span), f32),
+            pltpu.VMEM((plane, 8, span), f32),
+            dma((2, chips)),
+            dma((2, chips)),
+            dma((2, chips)),
+            dma((2, chips + 1)),
+            dma((row, 1, 3)),
+            dma((row, 1)),
+            dma((4, 4)),
+            dma((4, 4)),
+            dma((3, 2)),
+            dma((4,)),
+            dma((row,)),
+            dma((row,)),
+            dma((4,)),
+            dma((4,)),
+            dma((9,)),
+        ],
+        compiler_params=pltpu.CompilerParams(
+            collective_id=1, has_side_effects=True, vmem_limit_bytes=62 * 1024 * 1024
+        ),
+    )(x_all, cot_all, vec, bias, w_attn, attn_all, w_fc, w_proj, h1_all, qkv, w_qkv, lse, attn_own, ids_col, ids_row)
+
+
+def block_places(own, columns, width, span):
     groups = -(-width // span)
     first, last = own_blocks(own, columns, width, span)
     place = lax.iota(jnp.int32, 4 * span)
     block, lane = first + place // span, place % span
     at = (block % groups) * span + lane
-    there = (block <= last) & (at < width)
-    source = jnp.where(there, (block // groups) * width + at - own * columns, -1)
+    source = (block // groups) * width + at - own * columns
+    there = (block <= last) & (at < width) & (source >= 0) & (source < columns)
+    return jnp.where(there, source, -1)
+
+
+def joined_blocks(blocks, own, columns, width):
+    span = blocks.shape[2]
+    source = block_places(own, columns, width, span)
+    chosen = lax.broadcasted_iota(jnp.int32, (4 * span, columns), 1) == source[:, None]
+    lanes = blocks.transpose(1, 0, 2).reshape(-1, 4 * span)
+    lanes = jnp.where(source[None, :] >= 0, lanes, jnp.zeros_like(lanes))
+    return jnp.dot(lanes, chosen.astype(jnp.bfloat16), preferred_element_type=jnp.float32)
+
+
+def column_blocks(shard, own, width, span):
+    columns = shard.shape[1]
+    source = block_places(own, columns, width, span)
     chosen = lax.broadcasted_iota(jnp.int32, (columns, 4 * span), 0) == source[None, :]
     cut = jnp.dot(shard, chosen.astype(jnp.bfloat16), preferred_element_type=jnp.float32)
     return cut.astype(jnp.bfloat16).reshape(-1, 4, span).transpose(1, 0, 2)
@@ -1027,95 +1743,25 @@
     proj_own = jnp.pad(proj_weight, ((0, extra), (0, 0)))
     w_attn = join_fsdp(join_seq(attn_out_weight, 1))
 
-    inputs_all, grad_out_all, small_all, hidden1, qkv, w_qkv, lse, attn_own, attn_all, w_fc, w_proj = (
+    x_all, cot_all, small_all, vec, ids_col, ids_row, h1, qkv, w_qkv, lse, attn_own, attn_all, w_fc, w_proj = (
         attention_phase(tokens[0], cotangent[0], small, blocks, fc_own, proj_own, reach)
     )
-    inputs_all = inputs_all.reshape(length, width)
-    grad_out_all = grad_out_all.reshape(length, width)
-    hidden1 = hidden1.reshape(length, width)
-    w_fc, w_proj = w_fc.reshape(-1, width), w_proj.reshape(-1, width)
-    vector_rows = small_all[:, :, :2, :share].transpose(0, 2, 1, 3).reshape(-1, width)
     own_small = lax.dynamic_index_in_dim(small_all, own, 1, keepdims=False)
-    fc_shift = jnp.pad(own_small[:, 2, :units], ((0, 0), (0, extra))).reshape(-1)
-    ids_all = lax.dynamic_index_in_dim(small_all, lax.axis_index("fsdp"), 0, keepdims=False)
-    ids_all = ids_all[:, 3, :own_rows].reshape(length)
-    ids_col, ids_row = ids_all[:, None], ids_all[None, :]
-    attn_bf = attn_all[:, :width]
-
-    def own_tokens(values):
-        return lax.dynamic_slice_in_dim(values, own * own_rows, own_rows)
-
-    resid = (
-        inputs_all.astype(jnp.float32)
-        + jnp.dot(attn_bf, w_attn, preferred_element_type=jnp.float32)
-        + vector_rows[4]
-    )
-
-    normed2, inverse2, shifted2 = layer_norm(resid, vector_rows[5], vector_rows[6])
-    hidden2 = shifted2.astype(jnp.bfloat16)
-    preact = contract_last(hidden2, w_fc) + fc_shift
-    gelu_value, gelu_slope = gelu_parts(preact)
-    act_bf = gelu_value.astype(jnp.bfloat16)
-    grad_act = contract_last(grad_out_all, w_proj)
-    grad_pre = grad_act * gelu_slope
-    grad_pre_bf = grad_pre.astype(jnp.bfloat16)
-    grad_hidden2 = sum_seq(jnp.dot(grad_pre_bf, w_fc, preferred_element_type=jnp.float32))
-    result = (
-        own_tokens(resid)
-        + sum_seq(jnp.dot(act_bf, w_proj, preferred_element_type=jnp.float32))
-        + vector_rows[7]
-    )
-    own_proj = sum_fsdp(contract_first(act_bf, grad_out_all))[:units]
-    own_fc = sum_fsdp(contract_first(grad_pre_bf, hidden2))[:units].T
-    own_bias = sum_fsdp(jnp.sum(grad_pre, axis=0))[:units]
-
-    grad_out = cotangent[0].astype(jnp.float32)
-    grad_resid_norm, gain2_grad, shift2_grad = norm_back(
-        grad_hidden2, own_tokens(normed2), own_tokens(inverse2), vector_rows[5]
-    )
-    grad_resid = grad_out + grad_resid_norm
-    grad_resid_all = join_seq(grad_resid.astype(jnp.bfloat16))
-    padded_rows = jnp.pad(w_attn, ((0, 8 * span - width), (0, 0)))
-    attn_rows = lax.dynamic_slice_in_dim(padded_rows, group * span, span)
-    grad_attn = contract_last(grad_resid_all, attn_rows).astype(jnp.bfloat16)
-    grad_qkv = attention_backward(qkv, attn_own, grad_attn, lse, ids_col, ids_row, reach)
-    grad_qkv_bf = grad_qkv.astype(jnp.bfloat16)
-    grad_hidden1 = sum_seq(contract_last(grad_qkv_bf, w_qkv))
-    normed1, inverse1, _ = layer_norm(tokens[0].astype(jnp.float32), vector_rows[0], vector_rows[1])
-    grad_input_norm, gain1_grad, shift1_grad = norm_back(
-        grad_hidden1, normed1, inverse1, vector_rows[0]
-    )
-    input_grad = grad_resid + grad_input_norm
-
-    out_columns = attn_out_weight.shape[1]
-    own_columns = lax.dynamic_slice_in_dim(grad_resid_all, own * out_columns, out_columns, axis=1)
-    own_attn = sum_fsdp(contract_first(attn_bf, own_columns))
-    qkv_terms = sum_fsdp(contract_first(hidden1, grad_qkv_bf)).astype(jnp.bfloat16)
-    spread = lax.all_gather(qkv_terms, "seq", axis=0).reshape(parts, -1, 3, span)
-    natural = jnp.concatenate(
-        [spread[i] for i in (0, 1, 2, 4, 6, 7)] + [spread[3, :, :, : width % span]], axis=2
-    ).reshape(-1, 3 * width)
-    columns = qkv_weight.shape[1]
-    own_qkv = lax.dynamic_slice_in_dim(natural, own * columns, columns, axis=1).astype(jnp.float32)
-
-    def at_own_lanes(sums):
-        padded = jnp.zeros((8 * span,), jnp.float32)
-        return lax.dynamic_update_slice_in_dim(padded, sums, group * span, 0)[:width]
-
-    column_sums = jnp.sum(grad_qkv, axis=0)
-    vector_grad = jnp.stack(
-        [
-            gain1_grad,
-            shift1_grad,
-            at_own_lanes(column_sums[:span]),
-            at_own_lanes(column_sums[2 * span :]),
-            jnp.sum(grad_resid, axis=0),
-            gain2_grad,
-            shift2_grad,
-            jnp.sum(grad_out, axis=0),
-        ]
-    )
-    own_vec = sum_fsdp(sum_seq(vector_grad, 1))
+    bias = jnp.pad(own_small[:, 2], ((0, 4), (0, 0)))
+    w_attn = jnp.pad(w_attn, ((0, 8 * span - width), (0, 0)))
+    result, input_grad, fc_terms, proj_terms, attn_terms, nat_blocks, vec_sums, _ = backward_phase(
+        x_all, cot_all, vec, bias, w_attn, attn_all, w_fc, w_proj, h1, qkv, w_qkv, lse, attn_own, ids_col, ids_row, reach
+    )
+
+    def added(terms):
+        return jnp.sum(terms.astype(jnp.float32), axis=0)
+
+    own_qkv = joined_blocks(nat_blocks, own, qkv_weight.shape[1], width)
+    own_attn = added(attn_terms)[:, : attn_out_weight.shape[1]]
+    own_fc = added(fc_terms)[:units].T
+    own_proj = added(proj_terms)[:units]
+    own_vec = vec_sums[:2, :share]
+    own_bias = vec_sums[2, :units]
     return (result[None], input_grad[None], own_qkv, own_attn, own_fc, own_proj, own_vec, own_bias)
 
 

time: 725 us -> 389 us (0.54); the launches traced: 717 us -> 389 us
  waiting for transfers between devices: 343 us -> 29.3 us
  Pallas kernels: 138 us -> 308 us
  matrix products: 71.2 us -> 2.84 us
  local copies, waits for them, and re-layouts: 86.5 us -> 29 us
  blocking collectives: 37.9 us -> 0 us
  other arithmetic: 21.8 us -> 5.03 us
    pallas_call x1, Pallas kernels: 11.7 us -> 181 us  [backward_phase(): pl.pallas_call(lambda *refs: backward_kernel(reach, *refs), out_shape=[sh...]
    reduce_scatter x5 -> x0, waiting for transfers between devices: 152 us -> none  [the longest x3 128 us: sum_seq(): lax.psum_scatter(terms.astype(jnp.bfloat16), 'seq', scatter_dimension=axi...]
    unnamed x11 -> x2, waiting for transfers between devices: 115 us -> 0.03 us
    dot_general x11 -> x1, matrix products: 70.4 us -> 1.96 us  [joined_blocks(): jnp.dot(lanes, chosen.astype(jnp.bfloat16), preferred_element_type=jnp.fl...]
    all_gather x2 -> x1, waiting for transfers between devices: 67.3 us -> 29.2 us  [join_seq(): return lax.all_gather(block, 'seq', axis=axis, tiled=True)]
    unnamed x2 -> x0, blocking collectives: 37.9 us -> none
    reshape x3 -> x1, local copies, waits for them, and re-layouts: 25 us -> 1.24 us  [joined_blocks(): lanes = blocks.transpose(1, 0, 2).reshape(-1, 4 * span)]
    convert_element_type x3 -> x0, local copies, waits for them, and re-layouts: 16.4 us -> none  [sum_seq(): terms.astype(jnp.bfloat16)]
  transfers between devices with their start and end apart: 10 -> 2, of which waited for: 8 -> 1; matrix products, arithmetic and copies ran while one was open for 10% -> 1% of each run, Pallas kernels for 18% -> 33%
where the time goes in v2:
time: 389 us
  Pallas kernels  308 us (79%)
  waiting for transfers between devices  29.3 us (8%)
  local copies, waits for them, and re-layouts  29 us (7%)
  between operations  14.3 us (4%)
  other arithmetic  5.03 us (1%)
    pallas_call x1, Pallas kernels, backward_phase(): pl.pallas_call(lambda *refs: backward_kernel(reach, *refs), out_shape=[sh...  181 us
    pallas_call x1, Pallas kernels, attention_phase(): pl.pallas_call(lambda *refs: attention_kernel(reach, *refs), out_shape=[s...  127 us
    all_gather x1, waiting for transfers between devices, join_seq(): return lax.all_gather(block, 'seq', axis=axis, tiled=True)  29.2 us
    unnamed x35, local copies, waits for them, and re-layouts  11.1 us
  transfers between devices with their start and end apart: 2, of which 1 were waited for; matrix products, arithmetic and copies ran while one was open for 1% of the time, Pallas kernels for 33%

profile of v2, /device:TPU:0, one launch (start us, length us, event | category | flops | bytes accessed | tf_op | source)
XLA Modules:
  0.0 388.9 jit_solution(3123475914001278359)
XLA Ops:
  7.3 1.8 copy.33
  9.2 29.2 %all-gather.3.cloned.1.call-done = bf16[400,1600]{0,1:T(8,128)(2,1)} async-done(((bf16[400,200]{0,1:T(8,128)(2,1)}), bf16[400,1600]{0,1:T(8,128)(2,1)}) %all-gather.3.cloned.1.call-update) | async-done | bytes 1280016 | tf_op jit(solution)/shard_map/all_gather | solution.py:348
  38.4 3.5 copy.34
  43.0 0.9 pad.39.refs_5_
  43.9 0.9 fusion.2
  44.8 0.9 copy.42
  45.8 127.5 %shard_map.152 = (bf16[1024,1600]{1,0:T(8,128)(2,1)}, bf16[1024,1600]{1,0:T(8,128)(2,1)}, f32[4,8,8,256]{3,2,1,0:T(8,128)S(1)}, f32[8,2048]{1,0:T(8,128)S(1)}, f...) custom-call(bf16[128,1600]{1,0:T(8,128)(2,1)S(1)} %bitcast.26, ...), custom_call_target="tpu_custom_call" | custom-call | tf_op jit(solution)/shard_map/pallas_call | solution.py:865
  173.3 0.8 copy-done.2
  174.1 0.8 copy-done.3
  174.9 0.8 copy-done.4
  175.7 0.6 copy-done.5
  176.3 0.6 copy-done.6
  177.6 5.8 %pad.41.refs_4_ = bf16[2048,1600]{1,0:T(8,128)(2,1)} pad(bf16[1600,1600]{1,0:T(8,128)(2,1)} %all-gather.5.cloned.1.call-done, bf16[]{:T(256)} %constant.121.clone.1), padding=0_448x0_0 | pad | bytes 11673602 | tf_op jit(solution)/shard_map/jit(_pad)/pad | solution.py:1751
  183.4 180.8 %shard_map.153 = (f32[128,1600]{1,0:T(8,128)}, f32[128,1600]{1,0:T(8,128)}, bf16[4,208,1600]{2,1,0:T(8,128)(2,1)}, bf16[4,208,1600]{2,1,0:T(8,128)(2,1)}, bf16[4...) custom-call(bf16[1024,1600]{1,0:T(8,128)(2,1)} %get-tuple-element.29.ref, ...), custom_call_target="tpu_custom_call" | custom-call | tf_op jit(solution)/shard_map/pallas_call | solution.py:1626
  364.2 1.3 slice.23
  365.5 1.3 slice.22
  366.8 2.3 copy.36
  369.1 2.5 copy.37
  371.6 2.0 convert_reduce_fusion.2
  373.6 1.2 copy.39
  374.9 2.9 convert_reduce_fusion
  377.8 1.1 slice.27
  378.9 1.1 slice_bitcast_fusion
  380.1 2.0 fusion
  (44 shorter events, 1.8 us)
Async XLA Ops:
  7.2 36.7 %copy-start = (bf16[400,600]{1,0:T(8,128)(2,1)S(1)}, bf16[400,600]{1,0:T(8,128)(2,1)}, u32[]{:S(2)}) copy-start(bf16[400,600]{1,0:T(8,128)(2,1)} %param.12) | copy-start | bytes 1440004
  7.2 34.8 %copy-start.13 = (s32[1,128]{1,0:T(1,128)S(1)}, s32[1,128]{1,0:T(1,128)}, u32[]{:S(2)}) copy-start(s32[1,128]{1,0:T(1,128)} %param.10) | copy-start | bytes 1540
  7.2 34.8 %copy-start.14 = (bf16[200]{0:T(256)(128)(2,1)S(1)}, bf16[200]{0:T(256)(128)(2,1)}, u32[]{:S(2)}) copy-start(bf16[200]{0:T(256)(128)(2,1)} %param.17) | copy-start | bytes 1204
  7.2 34.8 %copy-start.10 = (bf16[1,128,1600]{1,2,0:T(8,128)(2,1)S(1)}, bf16[1,128,1600]{1,2,0:T(8,128)(2,1)}, u32[]{:S(2)}) copy-start(bf16[1,128,1600]{1,2,0:T(8,128)(2,1)} %param.9) | copy-start | bytes 1228804
  7.2 31.2 %all-gather.3.cloned.1.call-start = ((), (), s32[]{:S(2)}) async-start(), calls=%async_computation | async-start | bytes 1843200 | tf_op jit(solution)/shard_map/all_gather | solution.py:348
  9.1 33.2 %copy-start.11 = (bf16[1,128,1600]{1,2,0:T(8,128)(2,1)S(1)}, bf16[1,128,1600]{1,2,0:T(8,128)(2,1)}, u32[]{:S(2)}) copy-start(bf16[1,128,1600]{1,2,0:T(8,128)(2,1)} %param.11) | copy-start | bytes 1228804
  9.1 33.5 %copy-start.8 = (bf16[1600,200]{0,1:T(8,128)(2,1)S(1)}, bf16[1600,200]{0,1:T(8,128)(2,1)}, u32[]{:S(2)}) copy-start(bf16[1600,200]{0,1:T(8,128)(2,1)} %param.14) | copy-start | bytes 1920004
  9.1 168.5 %all-gather.5.cloned.1.call-start = ((), (), s32[]{:S(2)}) async-start(), calls=%async_computation.1 | async-start | bytes 6656000 | tf_op jit(solution)/shard_map/all_gather | solution.py:352
  41.9 1.1 copy-start.9
  43.9 1.9 copy-start.12
  173.3 0.8 copy-start.2
  174.1 0.8 copy-start.3
  174.9 0.8 copy-start.4
  175.7 0.6 copy-start.5
  176.3 0.6 copy-start.6
  369.1 5.8 %copy-start.7 = (bf16[4,208,1600]{2,1,0:T(8,128)(2,1)S(1)}, bf16[4,208,1600]{2,1,0:T(8,128)(2,1)}, u32[]{:S(2)}) copy-start(bf16[4,208,1600]{2,1,0:T(8,128)(2,1)} %get-tuple-element.47) | copy-start | bytes 7987204
  378.9 3.1 copy-start.1
Sparse Core Ops, SparseCore 0:
  10.3 28.1 all-gather.2
  42.0 99.6 all-gather.4

commit v3 on v2

--- a/solution.py
+++ b/solution.py
@@ -1,3 +1,4 @@
+import functools
 import math
 
 import jax
@@ -344,12 +345,15 @@
         yield start, first, start + tile - first
 
 
-def join_seq(block, axis=0):
-    return lax.all_gather(block, "seq", axis=axis, tiled=True)
-
-
-def join_fsdp(block, axis=0):
-    return lax.all_gather(block, "fsdp", axis=axis, tiled=True)
+norm_part = 32
+
+
+def row_tiles(count, size, body):
+    def step(i, carry):
+        body(pl.multiple_of(i * size, size))
+        return carry
+
+    lax.fori_loop(0, count // size, step, 0)
 
 
 MESH = pl.DeviceIdType.MESH
@@ -415,23 +419,25 @@
         self.when(i, c, backward, lambda: self.hop(i, c, 1, source).start())
         self.when(i, c, None, lambda: self.hop(i, c, 2, source).start())
 
-    def start(self):
-        for c in range(self.chunks):
+    def start(self, chunks=None):
+        for c in chunks or range(self.chunks):
             self.spread(
                 self.me, c, self.chip < self.chips - 1, self.chip > 0, self.own(c) if self.own else None
             )
 
-    def pass_on(self, distance):
+    def pass_on(self, distance, chunks=None):
+        chunks = chunks or range(self.chunks)
+
         def from_before():
             i = self.me - 2 * distance
-            for c in range(self.chunks):
+            for c in chunks:
                 self.when(i, c, None, lambda: self.hop(i, c, 2).wait_recv())
                 self.when(i, c, self.chip < self.chips - 1, lambda: self.hop(i, c, 0).start())
                 self.when(i, c, None, lambda: self.hop(i, c, 2).start())
 
         def from_after():
             i = self.me + 2 * distance
-            for c in range(self.chunks):
+            for c in chunks:
                 self.when(i, c, None, lambda: self.hop(i, c, 2).wait_recv())
                 self.when(i, c, self.chip > 0, lambda: self.hop(i, c, 1).start())
                 self.when(i, c, None, lambda: self.hop(i, c, 2).start())
@@ -439,11 +445,13 @@
         pl.when(self.chip >= distance)(from_before)
         pl.when(self.chip + distance < self.chips)(from_after)
 
+    def wait_other(self, i):
+        for c in range(self.chunks):
+            self.when(i, c, None, lambda: self.hop(i, c, 2).wait_recv())
+
     def from_other_core(self):
         for k in range(self.chips):
-            i = 2 * k + 1 - self.core
-            for c in range(self.chunks):
-                self.when(i, c, None, lambda: self.hop(i, c, 2).wait_recv())
+            self.wait_other(2 * k + 1 - self.core)
 
     def drain(self):
         for k in range(self.chips):
@@ -526,11 +534,15 @@
     return (centred * inverse) * gain + shift
 
 
-def attend(head, start, first, count, tile, qkv_ref, ids_col, ids_row, out_ref, lse_ref):
+def attend(head, pair, start, first, count, tile, qkv_ref, ids_col, ids_row, out_ref, lse_ref):
     span = out_ref.shape[1]
     rows, keys = pl.ds(start, tile), pl.ds(first, count)
-    query = only_head(qkv_ref[rows, :span], head)
-    scores = contract_last(query, qkv_ref[keys, span : 2 * span]) * (HEAD_DIM**-0.5)
+
+    def lanes(kind):
+        return pl.ds(kind * span + pair * 128, 128)
+
+    query = only_head(qkv_ref[rows, lanes(0)], head)
+    scores = contract_last(query, qkv_ref[keys, lanes(1)]) * (HEAD_DIM**-0.5)
     q_pos = start + lax.broadcasted_iota(jnp.int32, (tile, count), 0)
     k_pos = first + lax.broadcasted_iota(jnp.int32, (tile, count), 1)
     allowed = (k_pos <= q_pos) & (ids_col[rows, :1] == ids_row[:1, keys])
@@ -539,11 +551,11 @@
     weights = jnp.exp(masked - top)
     total = jnp.sum(weights, axis=1, keepdims=True)
     probs = (weights * (1.0 / total)).astype(jnp.bfloat16)
-    value = only_head(qkv_ref[keys, 2 * span :], head)
+    value = only_head(qkv_ref[keys, lanes(2)], head)
     mixed = jnp.dot(probs, value, preferred_element_type=jnp.float32)
-    out_ref[rows, :] += mixed.astype(jnp.bfloat16)
+    out_ref[rows, lanes(0)] += mixed.astype(jnp.bfloat16)
     lane = lax.broadcasted_iota(jnp.int32, (tile, lse_ref.shape[1]), 1)
-    lse_ref[rows, :] = jnp.where(lane == head, top + jnp.log(total), lse_ref[rows, :])
+    lse_ref[rows, :] = jnp.where(lane == 2 * pair + head, top + jnp.log(total), lse_ref[rows, :])
 
 
 def attention_kernel(
@@ -552,6 +564,7 @@
     cot_ref,
     small_ref,
     blocks_ref,
+    wo_ref,
     fc_ref,
     proj_ref,
     x_all,
@@ -568,6 +581,7 @@
     attn_all,
     fc_all,
     proj_all,
+    wo_all,
     x_v,
     small_v,
     vec,
@@ -578,6 +592,8 @@
     h1_v,
     qkv_v,
     attn_v,
+    wo_z,
+    wo_own,
     small_sent,
     small_landed,
     plane_sent,
@@ -596,6 +612,12 @@
     fc_landed,
     proj_sent,
     proj_landed,
+    wo_sent,
+    wo_landed,
+    wo_plane_sent,
+    wo_plane_landed,
+    wo_pair_sent,
+    wo_pair_landed,
     local_sem,
 ):
     row, plane = 8, 4
@@ -613,6 +635,8 @@
         copy.start()
         used.append(copy)
 
+    share = width // row
+
     vec[...] = jnp.zeros_like(vec)
     w_v[...] = jnp.zeros_like(w_v)
     greet(row, plane)
@@ -657,6 +681,23 @@
     own_x.start()
     used.append(None)
     x_line.start()
+
+    wo_line = RowGather(lambda c: wo_ref, lambda i, c: wo_z.at[i], wo_sent, wo_landed, row)
+    wo_line.start()
+    keep(wo_ref, wo_z.at[seq])
+    def slab(target):
+        def view(i, part):
+            start, count = (0, target.shape[1]) if part is None else part
+            return target.at[i, pl.ds(start, count)]
+
+        return view
+
+    units = fc_ref.shape[0]
+    cut = units // 32 * 16
+    parts = ((0, cut), (cut, units - cut))
+    fc_plane = PlaneGather(fc_ref, slab(fc_all), parts, fc_sent, fc_landed)
+    proj_plane = PlaneGather(proj_ref, slab(proj_all), parts, proj_sent, proj_landed)
+    fc_plane.start()
 
     for other in range(row):
         pltpu.make_async_copy(small_ref, small_v.at[fsdp, other], small_landed.at[other]).wait()
@@ -687,7 +728,6 @@
             "fsdp",
             lax.rem(fsdp + ahead, plane),
         ).wait_recv()
-    share = width // row
     for i in range(plane):
         for other in range(row):
             vec[2 * i : 2 * i + 2, share * other : share * (other + 1)] = small_v[i, other, 0:2, :share]
@@ -720,48 +760,106 @@
     half = depth // 32 * 16
     w_plane = PlaneGather(None, w_view, ((0, half), (half, depth - half)), w_sent, w_landed)
     w_plane.start()
+
+    def norm_block(i):
+        def part(j):
+            rows = pl.ds(pl.multiple_of(i * own_rows + j, norm_part), norm_part)
+            hidden = norm_rows(x_v[rows, :].astype(jnp.float32), vec[0:1, :width], vec[1:2, :width])
+            h1_v[rows, :] = hidden.astype(jnp.bfloat16)
+
+        row_tiles(own_rows, norm_part, part)
+
+    def norm_arrived(distance):
+        if 0 < distance < row // 2:
+            pl.when(x_line.chip >= distance)(lambda: norm_block(seq - 2 * distance))
+            pl.when(x_line.chip + distance < row // 2)(lambda: norm_block(seq + 2 * distance))
+
+        def other(i):
+            x_line.wait_other(i)
+            norm_block(i)
+
+        if distance == 1:
+            other(x_line.other)
+        elif distance > 1:
+            nearer = distance - 1
+            pl.when(x_line.chip >= nearer)(lambda: other(x_line.other - 2 * nearer))
+            pl.when(x_line.chip + nearer < row // 2)(lambda: other(x_line.other + 2 * nearer))
+
+    own_x.wait()
+    norm_block(seq)
     x_line.pass_on(1)
+    wo_line.pass_on(1)
+    norm_arrived(1)
     w_plane.pass_on()
-
-    def slab(target):
-        def view(i, part):
-            start, count = (0, target.shape[1]) if part is None else part
-            return target.at[i, pl.ds(start, count)]
-
-        return view
-
-    units = fc_ref.shape[0]
-    cut = units // 32 * 16
-    parts = ((0, cut), (cut, units - cut))
-    fc_plane = PlaneGather(fc_ref, slab(fc_all), parts, fc_sent, fc_landed)
-    proj_plane = PlaneGather(proj_ref, slab(proj_all), parts, proj_sent, proj_landed)
-    fc_plane.start()
-    proj_plane.start()
     x_line.pass_on(2)
+    wo_line.pass_on(2)
+    norm_arrived(2)
     x_line.pass_on(3)
+    wo_line.pass_on(3)
     cot_line = RowGather(lambda c: cot_ref, block_of(cot_all), cot_sent, cot_landed, row)
     cot_line.start()
+    norm_arrived(3)
     keep(cot_ref, block_of(cot_all)(seq, 0))
     keep(fc_ref, fc_all.at[fsdp])
     keep(proj_ref, proj_all.at[fsdp])
-    x_line.from_other_core()
-    own_x.wait()
+    norm_arrived(4)
     w_plane.finish()
+    fc_plane.pass_on()
+
+    wo_line.from_other_core()
+    used[1].wait()
+    used[1] = None
+    for i in range(row):
+        wo_own[:, share * i : share * (i + 1)] = wo_z[i]
+    wo_cut = 6 * 128
+    wo_lanes = ((0, wo_cut), (wo_cut, width - wo_cut))
+
+    def wo_view(lanes):
+        def view(i, part):
+            start, count = (0, depth) if part is None else part
+            rows = pl.ds(pl.multiple_of(i * depth + start, 16), count)
+            return wo_all.at[rows, pl.ds(*lanes)]
+
+        return view
+
+    wo_planes = [
+        PlaneGather(
+            wo_own.at[:, pl.ds(*lanes)],
+            wo_view(lanes),
+            ((0, half), (half, depth - half)),
+            wo_plane_sent,
+            wo_plane_landed,
+        )
+        for lanes in wo_lanes
+    ]
+
+    def wo_pair(core, ahead):
+        i = lax.rem(fsdp + ahead, plane)
+        place = wo_view(wo_lanes[core])(i, None)
+        return remote(place, place, wo_pair_sent.at[i], wo_pair_landed.at[i], "seq", x_line.other)
+
+    def wo_pairs(action, core):
+        for ahead in range(1, plane):
+            action(wo_pair(core, ahead))
+
+    def on_own_core(action):
+        for core in range(2):
+            pl.when(x_line.core == core)(functools.partial(action, core))
+
+    on_own_core(lambda core: wo_planes[core].start())
+    proj_plane.start()
+    keep(wo_own, wo_view((0, width))(fsdp, None))
     lanes = pl.ds(pl.multiple_of(group * span, span), span)
     query_shift, value_shift = vec[2:3, lanes], vec[3:4, lanes]
 
-    def project(i, carry):
-        rows = pl.ds(pl.multiple_of(i * own_rows, own_rows), own_rows)
-        hidden = norm_rows(x_v[rows, :].astype(jnp.float32), vec[0:1, :width], vec[1:2, :width])
-        hidden = hidden.astype(jnp.bfloat16)
-        h1_v[rows, :] = hidden
-        mixed = jnp.dot(hidden, w_v[...], preferred_element_type=jnp.float32)
+    def project(i):
+        rows = pl.ds(i, 2 * own_rows)
+        mixed = jnp.dot(h1_v[rows, :], w_v[...], preferred_element_type=jnp.float32)
         qkv_v[rows, :span] = (mixed[:, :span] + query_shift).astype(jnp.bfloat16)
         qkv_v[rows, span : 2 * span] = mixed[:, span : 2 * span].astype(jnp.bfloat16)
         qkv_v[rows, 2 * span :] = (mixed[:, 2 * span :] + value_shift).astype(jnp.bfloat16)
-        return carry
-
-    lax.fori_loop(0, row, project, 0)
+
+    row_tiles(length, 2 * own_rows, project)
     cot_line.pass_on(1)
     keep(x_v, x_all)
     keep(small_v, small_all)
@@ -776,14 +874,15 @@
     lse_all[...] = jnp.zeros_like(lse_all)
     tile = 256
 
-    def heads(h, carry):
-        for start, first, count in tile_pairs(length, tile, reach):
-            attend(h, start, first, count, tile, qkv_v, ids_col, ids_row, attn_v, lse_all)
-        return carry
-
-    lax.fori_loop(0, 2, heads, 0)
-    cot_line.pass_on(2)
-    lax.fori_loop(2, 4, heads, 0)
+    def heads(pair):
+        def head(h, carry):
+            for start, first, count in tile_pairs(length, tile, reach):
+                attend(h, pair, start, first, count, tile, qkv_v, ids_col, ids_row, attn_v, lse_all)
+            return carry
+
+        lax.fori_loop(0, 2, head, 0)
+
+    heads(0)
 
     def chunk(i, c):
         return attn_all.at[:, pl.ds(pl.multiple_of(group_of(i) * span + c * 128, 128), 128)]
@@ -797,36 +896,38 @@
         chunks=2,
         has=lambda i, c: group_of(i) < groups - c,
     )
-    attn_line.start()
-    for c in range(2):
+    def own_chunk(c):
         lanes = pl.ds(pl.multiple_of(group * span + c * 128, 128), 128)
-
-        @pl.when(group < groups - c)
-        def _():
-            pltpu.make_async_copy(
-                attn_v.at[:, pl.ds(c * 128, 128)], attn_all.at[:, lanes], piece_landed.at[c, 0]
-            ).start()
-
+        return pltpu.make_async_copy(
+            attn_v.at[:, pl.ds(c * 128, 128)], attn_all.at[:, lanes], piece_landed.at[c, 0]
+        )
+
+    def send_chunk(c):
+        attn_line.start([c])
+        pl.when(group < groups - c)(lambda: own_chunk(c).start())
+
+    send_chunk(0)
+    fc_plane.finish()
+    on_own_core(lambda core: wo_planes[core].pass_on())
+    heads(1)
+    send_chunk(1)
     keep(attn_v, attn_own_out)
-    fc_plane.pass_on()
-    proj_plane.pass_on()
+    for distance in range(1, row // 2):
+        attn_line.pass_on(distance, [0])
+        attn_line.pass_on(distance, [1])
+        if distance == 2:
+            proj_plane.pass_on()
+            on_own_core(lambda core: wo_planes[core].finish())
+            on_own_core(lambda core: wo_pairs(lambda copy: copy.start(), core))
+    cot_line.pass_on(2)
     cot_line.pass_on(3)
-    for distance in range(1, row // 2):
-        attn_line.pass_on(distance)
     attn_line.from_other_core()
     cot_line.from_other_core()
-    fc_plane.finish()
+    on_own_core(lambda core: wo_pairs(lambda copy: copy.wait_recv(), 1 - core))
     proj_plane.finish()
 
     for c in range(2):
-        lanes = pl.ds(pl.multiple_of(group * span + c * 128, 128), 128)
-
-        @pl.when(group < groups - c)
-        def _():
-            pltpu.make_async_copy(
-                attn_v.at[:, pl.ds(c * 128, 128)], attn_all.at[:, lanes], piece_landed.at[c, 0]
-            ).wait()
-
+        pl.when(group < groups - c)(lambda: own_chunk(c).wait())
     for ahead in range(1, row):
         small_to(lax.rem(seq + ahead, row), ahead - 1).wait_send()
     for ahead in range(1, plane):
@@ -838,8 +939,10 @@
         def _():
             remote(blocks_ref.at[k], place, piece_sent.at[k], landed, "seq", target).wait_send()
 
-    for line in (x_line, cot_line, attn_line, w_plane, fc_plane, proj_plane):
+    for line in (x_line, wo_line, cot_line, attn_line, w_plane, fc_plane, proj_plane):
         line.drain()
+    on_own_core(lambda core: wo_planes[core].drain())
+    on_own_core(lambda core: wo_pairs(lambda copy: copy.wait_send(), core))
     for copy in used:
         if copy is not None:
             copy.wait()
@@ -849,7 +952,7 @@
     return 3 * width // row
 
 
-def attention_phase(x_own, cot_own, small, blocks, fc_own, proj_own, reach):
+def attention_phase(x_own, cot_own, small, blocks, wo_own, fc_own, proj_own, reach):
     own_rows, width = x_own.shape
     row, plane, span = 8, 4, 256
     length = own_rows * row
@@ -879,9 +982,10 @@
             shaped(length, 7 * span),
             shaped(plane, units, width),
             shaped(plane, units, width),
+            shaped(8 * span, width),
         ],
-        in_specs=[anywhere] * 6,
-        out_specs=[anywhere] * 9 + [in_vmem] + [anywhere] * 4,
+        in_specs=[anywhere] * 7,
+        out_specs=[anywhere] * 9 + [in_vmem] + [anywhere] * 5,
         scratch_shapes=[
             pltpu.VMEM((length, width), bf),
             pltpu.VMEM((plane, row, 8, span), f32),
@@ -893,6 +997,8 @@
             pltpu.VMEM((length, width), bf),
             pltpu.VMEM((length, 3 * span), bf),
             pltpu.VMEM((length, span), bf),
+            pltpu.VMEM((row,) + wo_own.shape, bf),
+            pltpu.VMEM((width // plane, width), bf),
             dma((row - 1,)),
             dma((row,)),
             dma((plane - 1,)),
@@ -911,12 +1017,18 @@
             dma((4,)),
             dma((4,)),
             dma((4,)),
-            dma((16,)),
+            dma((row, 1, 3)),
+            dma((row, 1)),
+            dma((4,)),
+            dma((4,)),
+            dma((4,)),
+            dma((4,)),
+            dma((20,)),
         ],
         compiler_params=pltpu.CompilerParams(
             collective_id=0, has_side_effects=True, vmem_limit_bytes=50 * 1024 * 1024
         ),
-    )(x_own, cot_own, small, blocks, fc_own, proj_own)
+    )(x_own, cot_own, small, blocks, wo_own, fc_own, proj_own)
 
 
 def pick(index, values):
@@ -1081,14 +1193,6 @@
     )
     out_ref[keys, span : 2 * span] += scale * contract_first(score_grad, query)
     out_ref[keys, 2 * span :] += contract_first(probs.astype(jnp.bfloat16), grad)
-
-
-def row_tiles(count, size, body):
-    def step(i, carry):
-        body(pl.multiple_of(i * size, size))
-        return carry
-
-    lax.fori_loop(0, count // size, step, 0)
 
 
 def backward_kernel(
@@ -1213,8 +1317,19 @@
         bias_sum[...] = jnp.zeros_like(bias_sum)
         gv[...] = jnp.zeros_like(gv)
         greet(row, plane)
-        for copy in loads:
+        for copy in loads[:4]:
             copy.wait()
+
+        def back_through(rows, values, weights):
+            for low, high in tiles:
+                terms = jnp.dot(
+                    values[0, rows, :], weights[0, :, low:high], preferred_element_type=f32
+                )
+                for f in range(1, plane):
+                    terms += jnp.dot(
+                        values[f, rows, :], weights[f, :, low:high], preferred_element_type=f32
+                    )
+                wide[:, low:high] = terms
 
         def chunk(p, carry):
             t = chip_order(chip, p)
@@ -1229,13 +1344,13 @@
                 pltpu.make_async_copy(x_ref.at[rows], x_v, load_sem.at[2]).wait()
 
             def second_norm(i):
-                part = pl.ds(i, 16)
+                part = pl.ds(i, norm_part)
                 resid = wide[part, :] + x_v[part, :].astype(f32) + vec_v[4:5, :width]
                 wide[part, :] = resid
                 hidden = norm_rows(resid, vec_v[5:6, :width], vec_v[6:7, :width])
-                h2_v[pl.ds(pl.multiple_of(t * pair_rows + i, 16), 16), :] = hidden.astype(bf)
-
-            row_tiles(pair_rows, 16, second_norm)
+                h2_v[pl.ds(pl.multiple_of(t * pair_rows + i, norm_part), norm_part), :] = hidden.astype(bf)
+
+            row_tiles(pair_rows, norm_part, second_norm)
 
             @pl.when(p < chips - 1)
             def _():
@@ -1262,31 +1377,23 @@
                 row_tiles(pair_rows, 32, gelu)
                 return carry
 
+            @pl.when(p == 0)
+            def _():
+                for copy in loads[4:]:
+                    copy.wait()
+
             lax.fori_loop(0, plane, unit_block, 0)
 
-            def back_through(values, weights):
-                for low, high in tiles:
-                    terms = jnp.dot(
-                        values[0, rows, :], weights[0, :, low:high], preferred_element_type=f32
-                    )
-                    for f in range(1, plane):
-                        terms += jnp.dot(
-                            values[f, rows, :], weights[f, :, low:high], preferred_element_type=f32
-                        )
-                    wide[:, low:high] = terms
-
-            back_through(dpre_v, fc_v)
+            back_through(rows, dpre_v, fc_v)
             hidden_sum.put(t, wide)
-            back_through(act_v, proj_v)
-            out_sum.put(t, wide)
 
             @pl.when(ends & (p < chips - 1))
             def _():
                 hidden_sum.step(t)
 
-            @pl.when(jnp.logical_not(ends) & (p == 2))
+            @pl.when(jnp.logical_not(ends) & (p > 0) & (p < chips - 1))
             def _():
-                hidden_sum.step(chip_order(chip, 0))
+                hidden_sum.step(chip_order(chip, p - 1))
 
             return carry
 
@@ -1294,13 +1401,12 @@
 
         @pl.when(jnp.logical_not(ends))
         def _():
-            hidden_sum.step(chip_order(chip, 1))
             hidden_sum.step(chip_order(chip, 2))
 
         hidden_sum.final(total)
 
         def second_norm_back(i):
-            part = pl.ds(i, 16)
+            part = pl.ds(i, norm_part)
             resid = resid_own[part, :]
             centred = resid - jnp.mean(resid, axis=-1, keepdims=True)
             inverse = lax.rsqrt(jnp.mean(centred * centred, axis=-1, keepdims=True) + norm_eps)
@@ -1312,7 +1418,7 @@
                 - jnp.mean(scaled, axis=-1, keepdims=True)
                 - normed * jnp.mean(scaled * normed, axis=-1, keepdims=True)
             )
-            place = pl.ds(pl.multiple_of(seq * own_rows + i, 16), 16)
+            place = pl.ds(pl.multiple_of(seq * own_rows + i, norm_part), norm_part)
             cot = cot_v[place, :].astype(f32)
             grad_resid = cot + back
             dresid_own[part, :] = grad_resid
@@ -1320,13 +1426,19 @@
             for at, values in ((4, grad_resid), (5, grad_hidden * normed), (6, grad_hidden), (7, cot)):
                 gv[at : at + 1, :width] += jnp.sum(values, axis=0, keepdims=True)
 
-        row_tiles(own_rows, 16, second_norm_back)
+        row_tiles(own_rows, norm_part, second_norm_back)
         dr_line.start()
 
-        @pl.when(ends)
-        def _():
-            for p in range(chips - 1):
-                out_sum.step(chip_order(chip, p))
+        def out_chunk(p, carry):
+            t = chip_order(chip, p)
+            back_through(pair_at(t), act_v, proj_v)
+            out_sum.put(t, wide)
+
+            @pl.when(ends & (p < chips - 1))
+            def _():
+                out_sum.step(t)
+
+            return carry
 
         def weight_terms(values, others, stage):
             def unit_block(f, carry):
@@ -1338,9 +1450,10 @@
 
         weight_terms(act_v, cot_v, proj_stage)
         proj_plane.start()
-        dr_line.pass_on(1)
         weight_terms(dpre_v, h2_v, fc_stage)
         fc_plane.start()
+        dr_line.pass_on(1)
+        lax.fori_loop(0, chips, out_chunk, 0)
         dr_line.pass_on(2)
 
     pl.run_scoped(
@@ -1372,8 +1485,11 @@
         dqkv[...] = jnp.zeros_like(dqkv)
         dr_line.pass_on(3)
         dr_line.from_other_core()
-        for copy in loads:
+        for copy in loads[:6]:
             copy.wait()
+
+        inside = lax.broadcasted_iota(jnp.int32, w_rows.shape, 0) < width - group * span
+        w_rows[...] = jnp.where(inside, w_rows[...], jnp.zeros_like(w_rows))
 
         def into_heads(i):
             rows = pl.ds(i, pair_rows)
@@ -1409,6 +1525,8 @@
         gv[3:4, lanes] = jnp.sum(dqkv[:, 2 * span :], axis=0, keepdims=True)
         dqkv16[...] = dqkv[...].astype(bf)
 
+        for copy in loads[6:]:
+            copy.wait()
         for low in range(0, width, span):
             high = min(low + span, width)
             gq[low:high, :] = contract_first(h1_v[:, low:high], dqkv16[...]).astype(bf)
@@ -1462,6 +1580,12 @@
             for p in range(chips - 1):
                 hidden_sum.step(chip_order(chip, p))
 
+        out_sum.final(total)
+        for low, high in tiles:
+            result_ref[:, low:high] = (
+                resid_own[:, low:high] + total[:, low:high] + vec_v[7:8, low:high]
+            )
+
         qkv_plane.arrive()
         load(qkv_terms, gqt, 0).wait()
         qkv_plane.drain()
@@ -1509,7 +1633,7 @@
         hidden_sum.final(total)
 
         def first_norm_back(i):
-            part = pl.ds(i, 16)
+            part = pl.ds(i, norm_part)
             values = own_x[part, :].astype(f32)
             centred = values - jnp.mean(values, axis=-1, keepdims=True)
             inverse = lax.rsqrt(jnp.mean(centred * centred, axis=-1, keepdims=True) + norm_eps)
@@ -1525,7 +1649,7 @@
             for at, summed in ((0, grad_hidden * normed), (1, grad_hidden)):
                 gv[at : at + 1, :width] += jnp.sum(summed, axis=0, keepdims=True)
 
-        row_tiles(own_rows, 16, first_norm_back)
+        row_tiles(own_rows, norm_part, first_norm_back)
 
         vec_send[...] = jnp.zeros_like(vec_send)
         plane_send[...] = jnp.zeros_like(plane_send)
@@ -1542,11 +1666,6 @@
         keep.start()
         for ahead in range(1, row):
             vec_to(ahead).start()
-        out_sum.final(total)
-        for low, high in tiles:
-            result_ref[:, low:high] = (
-                resid_own[:, low:high] + total[:, low:high] + vec_v[7:8, low:high]
-            )
         for i in range(row):
             pltpu.make_async_copy(vec_send.at[i], vec_land.at[i], vec_landed.at[i]).wait()
         summed = vec_land[0]
@@ -1741,14 +1860,12 @@
     blocks = column_blocks(qkv_weight, own, width, span)
     fc_own = jnp.pad(fc_weight.T, ((0, extra), (0, 0)))
     proj_own = jnp.pad(proj_weight, ((0, extra), (0, 0)))
-    w_attn = join_fsdp(join_seq(attn_out_weight, 1))
-
-    x_all, cot_all, small_all, vec, ids_col, ids_row, h1, qkv, w_qkv, lse, attn_own, attn_all, w_fc, w_proj = (
-        attention_phase(tokens[0], cotangent[0], small, blocks, fc_own, proj_own, reach)
+
+    x_all, cot_all, small_all, vec, ids_col, ids_row, h1, qkv, w_qkv, lse, attn_own, attn_all, w_fc, w_proj, w_attn = (
+        attention_phase(tokens[0], cotangent[0], small, blocks, attn_out_weight, fc_own, proj_own, reach)
     )
     own_small = lax.dynamic_index_in_dim(small_all, own, 1, keepdims=False)
     bias = jnp.pad(own_small[:, 2], ((0, 4), (0, 0)))
-    w_attn = jnp.pad(w_attn, ((0, 8 * span - width), (0, 0)))
     result, input_grad, fc_terms, proj_terms, attn_terms, nat_blocks, vec_sums, _ = backward_phase(
         x_all, cot_all, vec, bias, w_attn, attn_all, w_fc, w_proj, h1, qkv, w_qkv, lse, attn_own, ids_col, ids_row, reach
     )

time: 389 us -> 320 us (0.82)
  waiting for transfers between devices: 29.3 us -> 0 us
  Pallas kernels: 308 us -> 293 us
  between operations: 14.3 us -> 0.87 us
  local copies, waits for them, and re-layouts: 29 us -> 20.1 us
    all_gather x2 -> x0, waiting for transfers between devices: 29.3 us -> none  [the longest x1 29.2 us: join_seq(): return lax.all_gather(block, 'seq', axis=axis, tiled=True)]
    pallas_call x1, Pallas kernels: 181 us -> 168 us  [backward_phase(): pl.pallas_call(lambda *refs: backward_kernel(reach, *refs), out_shape=[sh...]
    pad x1 -> x0, local copies, waits for them, and re-layouts: 5.83 us -> none  [token_plan(): w_attn = jnp.pad(w_attn, ((0, 8 * span - width), (0, 0)))]
    unnamed x35 -> x28, local copies, waits for them, and re-layouts: 11.1 us -> 10.9 us
  transfers between devices with their start and end apart: 2 -> 0, of which waited for: 1 -> 0; matrix products, arithmetic and copies ran while one was open for 1% -> 0% of each run, Pallas kernels for 33% -> 0%
where the time goes in v3:
time: 320 us
  Pallas kernels  293 us (92%)
  local copies, waits for them, and re-layouts  20.1 us (6%)
    pallas_call x1, Pallas kernels, backward_phase(): pl.pallas_call(lambda *refs: backward_kernel(reach, *refs), out_shape=[sh...  168 us
    pallas_call x1, Pallas kernels, attention_phase(): pl.pallas_call(lambda *refs: attention_kernel(reach, *refs), out_shape=[s...  125 us
    unnamed x28, local copies, waits for them, and re-layouts  10.9 us

profile of v3, /device:TPU:0, one launch (start us, length us, event | category | flops | bytes accessed | tf_op | source)
XLA Modules:
  0.0 319.8 jit_solution(15325558570323438047)
XLA Ops:
  0.8 0.8 convert_element_type.33
  1.5 0.7 broadcast_in_dim.27
  2.2 0.7 pad_convert_fusion.1
  3.0 1.2 copy.22
  4.2 1.2 copy.23
  5.4 1.1 pad.34.refs_5_
  6.6 0.9 pad.35.refs_6_
  7.5 0.9 fusion.2
  8.4 0.9 copy.33
  9.3 125.2 %shard_map.152 = (bf16[1024,1600]{1,0:T(8,128)(2,1)}, bf16[1024,1600]{1,0:T(8,128)(2,1)}, f32[4,8,8,256]{3,2,1,0:T(8,128)S(1)}, f32[8,2048]{1,0:T(8,128)S(1)}, f...) custom-call(bf16[128,1600]{1,0:T(8,128)(2,1)S(1)} %bitcast.26, ...), custom_call_target="tpu_custom_call" | custom-call | tf_op jit(solution)/shard_map/pallas_call | solution.py:968
  134.6 0.8 copy-done.1
  135.4 0.8 copy-done.2
  136.2 0.8 copy-done.3
  137.0 0.6 copy-done.5
  138.8 167.5 %shard_map.153 = (f32[128,1600]{1,0:T(8,128)}, f32[128,1600]{1,0:T(8,128)}, bf16[4,208,1600]{2,1,0:T(8,128)(2,1)}, bf16[4,208,1600]{2,1,0:T(8,128)(2,1)}, bf16[4...) custom-call(bf16[1024,1600]{1,0:T(8,128)(2,1)} %get-tuple-element.30.ref, ...), custom_call_target="tpu_custom_call" | custom-call | tf_op jit(solution)/shard_map/pallas_call | solution.py:1745
  306.4 2.5 copy.27
  308.8 2.3 copy.28
  311.2 1.3 slice.23
  312.4 1.3 slice.22
  313.7 0.9 convert_reduce_fusion.2
  314.7 2.0 fusion
  316.7 0.8 convert_reduce_fusion
  317.5 1.1 slice.27
  318.6 1.1 slice_bitcast_fusion
  (29 shorter events, 1.4 us)
Async XLA Ops:
  0.6 6.9 %copy-start = (bf16[400,600]{1,0:T(8,128)(2,1)S(1)}, bf16[400,600]{1,0:T(8,128)(2,1)}, u32[]{:S(2)}) copy-start(bf16[400,600]{1,0:T(8,128)(2,1)} %param.12) | copy-start | bytes 1440004
  0.6 6.0 %copy-start.11 = (bf16[200,1600]{1,0:T(8,128)(2,1)S(1)}, bf16[200,1600]{1,0:T(8,128)(2,1)}, u32[]{:S(2)}) copy-start(bf16[200,1600]{1,0:T(8,128)(2,1)} %param.15) | copy-start | bytes 1920004
  7.5 1.8 copy-start.4
  134.6 0.8 copy-start.1
  135.4 0.8 copy-start.2
  136.2 0.8 copy-start.3
  137.0 0.6 copy-start.5
  137.6 0.6 copy-start.6
  306.4 7.3 %copy-start.10 = (bf16[4,400,256]{2,1,0:T(8,128)(2,1)S(1)}, bf16[4,400,256]{2,1,0:T(8,128)(2,1)}, u32[]{:S(2)}) copy-start(bf16[4,400,256]{2,1,0:T(8,128)(2,1)} %get-tuple-element.48) | copy-start | bytes 2457604
  306.4 8.2 %copy-start.9 = (bf16[4,400,256]{2,1,0:T(8,128)(2,1)S(1)}, bf16[4,400,256]{2,1,0:T(8,128)(2,1)}, u32[]{:S(2)}) copy-start(bf16[4,400,256]{2,1,0:T(8,128)(2,1)} %get-tuple-element.47) | copy-start | bytes 2457604
  313.7 2.9 copy-start.8
  314.6 2.1 copy-start.7
